TPU v7x, 128 devices: a whole 4x4x4 slice. The times are simulated.
128 devices in a mesh: group: 8 (over x, y_lo), blk: 16 (over y_hi, z, core).
Axes of the slice: x: 4, y: 4 (y_hi: 2, y_lo: 2; y = y_hi * 2 + y_lo), z: 4, core: 2. Of those that a mesh axis runs over, the one named last changes fastest.
Arguments:
- spectra: bfloat16 [2048, 2, 2048], P(('group', 'blk')), may hold values from -6 to 6
- live_count: int32 [128], P(('group', 'blk')), may hold values from 12 to 16
- owner_list: int32 [262144, 1], P(('group', 'blk')), may hold values from 0 to 127; in each aligned block of 2048 rows (0 to 2047, 2048 to 4095, ...) at most 32 rows name the same one
- bin_list: int32 [262144], P(('group', 'blk')), may hold values from 0 to 63
Outputs:
- stacks: float32 [8192, 256], P(('group', 'blk'))
Inputs may be any that keep to these rules, and one draw needn't show every extreme that they name: `owner_list`: among the rows of one channel block, no owner is named by more than 32 rows, and some block names some owner exactly 32 times; every owner is named somewhere.
All inputs are finite; a program needn't handle non-finite values.
Results may differ from a plain program's by a relative error of at most 0.012.
Values may be sent and summed in bfloat16 or wider, within the bound.
A program may use at most 64 MiB of HBM per device.

v0:
```python
import math

import jax
import jax.numpy as jnp
from jax import lax
from jax.sharding import PartitionSpec as P

LAGS = 256
SMOOTH = 8
BINS_DEV = 64


def from_behind(value, axis, steps):
    count = lax.axis_size(axis)
    pairs = [(source, (source + steps) % count) for source in range(count)]
    return lax.ppermute(value, axis, pairs)


def whiten(block, live):
    values = block.astype(jnp.float32)
    energy = values[:, 0] * values[:, 0] + values[:, 1] * values[:, 1]
    width = energy.shape[1]
    smooth = jnp.mean(energy.reshape(energy.shape[0], width // SMOOTH, SMOOTH), axis=2)
    smooth = jnp.repeat(smooth, SMOOTH, axis=1)
    level = jnp.mean(energy, axis=1, keepdims=True)
    alive = (jnp.arange(energy.shape[0], dtype=jnp.int32) < live).astype(jnp.float32)
    inverse_amp = lax.rsqrt(smooth + 0.1 * level + 1e-06) * alive[:, None]
    return (values * inverse_amp[:, None, :]).astype(jnp.bfloat16)


def build_table(width, lag_count):
    frequency = jnp.arange(width, dtype=jnp.int32)
    lag_offset = jnp.arange(lag_count, dtype=jnp.int32) - lag_count // 2
    product = frequency[:, None] * lag_offset[None, :] % (2 * width)
    angles = product.astype(jnp.float32) * (math.pi / width)
    norm_factor = 1.0 / math.sqrt(width)
    return (jnp.concatenate([jnp.cos(angles), -jnp.sin(angles)], axis=0) * norm_factor).astype(
        jnp.bfloat16
    )


def correlate(own_block, far_block, lag_table):
    near_vals = own_block.astype(jnp.float32)
    far_vals = far_block.astype(jnp.float32)
    real_own, imag_own = (near_vals[:, 0][:, None, :], near_vals[:, 1][:, None, :])
    real_far, imag_far = (far_vals[:, 0][None, :, :], far_vals[:, 1][None, :, :])
    real_part = real_own * real_far + imag_own * imag_far
    imag_part = imag_own * real_far - real_own * imag_far
    cross_spec = jnp.concatenate([real_part, imag_part], axis=2).astype(jnp.bfloat16)
    pairs = cross_spec.shape[0] * cross_spec.shape[1]
    return jnp.dot(
        cross_spec.reshape(pairs, cross_spec.shape[2]),
        lag_table,
        preferred_element_type=jnp.float32,
    )


def on_device(spectra, live_count, owner_list, bin_list):
    own_block = whiten(spectra, live_count[0])
    lag_table = build_table(spectra.shape[2], LAGS)
    step_count = lax.axis_size("blk") // 2
    row_list = []
    travel = own_block
    for step in range(1, step_count + 1):
        travel = from_behind(travel, "blk", 1)
        row_list.append(correlate(own_block, travel, lag_table))
    lag_rows = jnp.concatenate(row_list, axis=0)
    n_group = lax.axis_size("group")
    n_blk = lax.axis_size("blk")
    devices = n_group * n_blk
    target = owner_list[:, 0]
    row_count = target.shape[0]
    capacity = max(2, 2 * row_count // devices)
    sort_order = jnp.argsort(target, stable=True)
    sorted_target = target[sort_order]
    counts = jnp.sum(
        (target[:, None] == jnp.arange(devices, dtype=jnp.int32)[None, :]).astype(jnp.int32), axis=0
    )
    starts = jnp.cumsum(counts) - counts
    rank_sorted = jnp.arange(row_count, dtype=jnp.int32) - starts[sorted_target]
    slot_index = (
        jnp.zeros((row_count,), jnp.int32)
        .at[sort_order]
        .set(sorted_target * capacity + rank_sorted)
    )
    row_buffer = jnp.zeros((devices * capacity, LAGS), jnp.float32).at[slot_index].set(lag_rows)
    bin_buffer = jnp.full((devices * capacity,), -1, jnp.int32).at[slot_index].set(bin_list)
    row_in, bin_in = (
        lax.all_to_all(
            row_buffer.reshape(devices, capacity, LAGS),
            ("group", "blk"),
            split_axis=0,
            concat_axis=0,
            tiled=True,
        ),
        lax.all_to_all(
            bin_buffer.reshape(devices, capacity),
            ("group", "blk"),
            split_axis=0,
            concat_axis=0,
            tiled=True,
        ),
    )
    row_in = row_in.reshape(devices * capacity, LAGS)
    bin_in = bin_in.reshape(devices * capacity)
    onehot = (jnp.arange(BINS_DEV, dtype=jnp.int32)[:, None] == bin_in[None, :]).astype(jnp.float32)
    stack_sums = jnp.dot(
        onehot, row_in, precision=lax.Precision.HIGHEST, preferred_element_type=jnp.float32
    )
    hits = jnp.sum(onehot, axis=1)
    return stack_sums / jnp.sqrt(hits + 1.0)[:, None]


def solution(mesh):
    return jax.shard_map(
        on_device,
        mesh=mesh,
        in_specs=(
            P(("group", "blk"), None, None),
            P(("group", "blk")),
            P(("group", "blk"), None),
            P(("group", "blk")),
        ),
        out_specs=P(("group", "blk"), None),
        check_vma=False,
    )
```

profile of v0, /device:TPU:0, one launch (start us, length us, event | category | flops | bytes accessed | tf_op | source)
XLA Modules:
  0.0 214.1 jit_solution(1343310549645260327)
XLA Ops:
  0.0 0.9 copy_convert_fusion
  3.5 5.0 %sort.17 = (s32[2048]{0:T(1024)}, s32[2048]{0:T(1024)S(1)}) sort(s32[2048]{0:T(1024)S(1)} %bitcast.75, s32[2048]{0:T(1024)S(1)} %iota.31), dimensions={0}, to_apply=%region_0.0 | sort | flops 22528 | bytes 32768 | tf_op jit(solution)/shard_map/jit(argsort)/sort | solution.py:74
  8.9 11.8 %gather_fusion = s32[2048]{0:T(1024)S(1)} fusion(s32[2048]{0:T(1024)S(1)} %bitcast.76, s32[2048]{0:T(1024)S(1)} %get-tuple-element.59), kind=kCustom, calls=%fused_computation | custom fusion | bytes 24576 | tf_op jit(solution)/shard_map/gather | solution.py:75
  20.7 12.6 %gather_fusion.1 = s32[2048]{0:T(1024)S(1)} fusion(s32[128]{0:T(128)S(1)} %sub.68, s32[2048]{0:T(1024)S(1)} %broadcast_clamp_fusion), kind=kCustom, calls=%fused_computation.1 | custom fusion | bytes 24576 | tf_op jit(solution)/shard_map/gather | solution.py:80
  33.4 8.0 %scatter_custom_fusion = s32[2048]{0:T(1024)S(1)} fusion(s32[2048]{0:T(1024)S(1)} %get-tuple-element.60, s32[2048]{0:T(1024)S(1)} %subtract_add_fusion, s32[]{:T(128)} %constant.16.clone.1), kind=kCustom, calls=%fused_computation.117 | custom fusion | bytes 8196 | tf_op jit(solution)/shard_map/scatter | solution.py:84
  41.5 8.2 %scatter_custom_fusion.1 = s32[4096]{0:T(1024)S(1)} fusion(s32[2048]{0:T(1024)S(1)} %compare_select_fusion.1, s32[2048]{0:T(1024)} %param.7, s32[]{:T(128)} %constant.15.clone.1), kind=kCustom, calls=%fused_computation.113 | custom fusion | bytes 16896 | tf_op jit(solution)/shard_map/scatter | solution.py:87
  49.7 0.7 all_to_all.9
  50.4 12.5 %all-to-all-start = ((s32[128,1,32]{2,1,0:T(1,128)}), s32[128,1,32]{2,1,0:T(1,128)S(1)}, u32[]{:S(2)}, u32[]{:S(2)}) async-start(s32[128,1,32]{2,1,0:T(1,128)} %bitcast.4), calls=%async_computation | async-start | bytes 131072 | tf_op jit(solution)/shard_map/all_to_all | solution.py:96
  62.9 8.2 %fusion.65 = (f32[2048,256]{1,0:T(8,128)S(1)}, f32[2048,256]{1,0:T(8,128)S(1)}) fusion(s32[256]{0:T(256)S(1)} %iota_add_fusion), kind=kLoop, calls=%fused_computation.78 | loop fusion | flops 7864320 | bytes 4195328 | tf_op jit(solution)/shard_map/cos | solution.py:37
  71.8 7.9 %collective-permute-done.1 = bf16[16,2,2048]{2,0,1:T(8,128)(2,1)S(1)} collective-permute-done((bf16[16,2,2048]{2,0,1:T(8,128)(2,1)S(1)}, bf16[16,2,2048]{2,0,1:T(8,128)(2,1)S(1)}, u32[]{:S(2)}, u32[]{:S(2)}) %collective-permute-start.1) | collective-permute-done | bytes 131104 | tf_op jit(solution)/shard_map/ppermute | solution.py:16
  79.8 8.0 %collective-permute-done.2 = bf16[16,2,2048]{2,0,1:T(8,128)(2,1)S(1)} collective-permute-done((bf16[16,2,2048]{2,0,1:T(8,128)(2,1)S(1)}, bf16[16,2,2048]{2,0,1:T(8,128)(2,1)S(1)}, u32[]{:S(2)}, u32[]{:S(2)}) %collective-permute-start.2) | collective-permute-done | bytes 131104 | tf_op jit(solution)/shard_map/ppermute | solution.py:16
  87.8 8.0 %collective-permute-done.3 = bf16[16,2,2048]{2,0,1:T(8,128)(2,1)S(1)} collective-permute-done((bf16[16,2,2048]{2,0,1:T(8,128)(2,1)S(1)}, bf16[16,2,2048]{2,0,1:T(8,128)(2,1)S(1)}, u32[]{:S(2)}, u32[]{:S(2)}) %collective-permute-start.3) | collective-permute-done | bytes 131104 | tf_op jit(solution)/shard_map/ppermute | solution.py:16
  95.8 8.0 %collective-permute-done.4 = bf16[16,2,2048]{2,0,1:T(8,128)(2,1)S(1)} collective-permute-done((bf16[16,2,2048]{2,0,1:T(8,128)(2,1)S(1)}, bf16[16,2,2048]{2,0,1:T(8,128)(2,1)S(1)}, u32[]{:S(2)}, u32[]{:S(2)}) %collective-permute-start.4) | collective-permute-done | bytes 131104 | tf_op jit(solution)/shard_map/ppermute | solution.py:16
  103.8 8.0 %collective-permute-done.5 = bf16[16,2,2048]{2,0,1:T(8,128)(2,1)S(1)} collective-permute-done((bf16[16,2,2048]{2,0,1:T(8,128)(2,1)S(1)}, bf16[16,2,2048]{2,0,1:T(8,128)(2,1)S(1)}, u32[]{:S(2)}, u32[]{:S(2)}) %collective-permute-start.5) | collective-permute-done | bytes 131104 | tf_op jit(solution)/shard_map/ppermute | solution.py:16
  111.8 8.0 %collective-permute-done.6 = bf16[16,2,2048]{2,0,1:T(8,128)(2,1)S(1)} collective-permute-done((bf16[16,2,2048]{2,0,1:T(8,128)(2,1)S(1)}, bf16[16,2,2048]{2,0,1:T(8,128)(2,1)S(1)}, u32[]{:S(2)}, u32[]{:S(2)}) %collective-permute-start.6) | collective-permute-done | bytes 131104 | tf_op jit(solution)/shard_map/ppermute | solution.py:16
  119.9 8.0 %collective-permute-done.7 = bf16[16,2,2048]{2,0,1:T(8,128)(2,1)S(1)} collective-permute-done((bf16[16,2,2048]{2,0,1:T(8,128)(2,1)S(1)}, bf16[16,2,2048]{2,0,1:T(8,128)(2,1)S(1)}, u32[]{:S(2)}, u32[]{:S(2)}) %collective-permute-start.7) | collective-permute-done | bytes 131104 | tf_op jit(solution)/shard_map/ppermute | solution.py:16
  127.9 5.3 %add_convert_fusion = (bf16[16,16,2048]{2,1,0:T(8,128)(2,1)S(1)}, bf16[16,16,2048]{2,1,0:T(8,128)(2,1)S(1)}, bf16[16,16,2048]{2,1,0:T(8,128)(2,1)S(1)}, bf16[16,...) fusion(f32[16,2048]{1,0:T(8,128)S(1)} %get-tuple-element.42, ...), kind=kLoop, calls=%fused_computation.46 | loop fusion | flops 33554432 | bytes 19136512 | tf_op jit(solution)/shard_map/convert.3
  133.9 0.7 fusion.59
  138.2 0.7 fusion.41
  138.9 11.2 %scatter_custom_fusion.2 = f32[4096,256]{1,0:T(8,128)} fusion(s32[2048]{0:T(1024)S(1)} %compare_select_fusion.1, f32[2048,256]{1,0:T(8,128)S(1)} %fusion.41, f32[]{:T(128)} %constant.14.clone.1), kind=kCustom, calls=%fused_computation.64 | custom fusion | bytes 4194308 | tf_op jit(solution)/shard_map/scatter | solution.py:86
  150.1 7.2 %all-to-all-start.1 = ((f32[128,32,256]{2,1,0:T(8,128)}), f32[128,32,256]{2,1,0:T(8,128)}, u32[]{:S(2)}, u32[]{:S(2)}) async-start(f32[128,32,256]{2,1,0:T(8,128)} %bitcast.77), calls=%async_computation.1 | async-start | bytes 8388608 | tf_op jit(solution)/shard_map/all_to_all | solution.py:89
  157.8 0.8 reduce.5
  158.9 50.5 %all-to-all-done.1 = f32[128,32,256]{2,1,0:T(8,128)} async-done(((f32[128,32,256]{2,1,0:T(8,128)}), f32[128,32,256]{2,1,0:T(8,128)}, u32[]{:S(2)}, u32[]{:S(2)}) %all-to-all-start.1) | async-done | bytes 4194336 | tf_op jit(solution)/shard_map/all_to_all | solution.py:89
  209.5 4.6 %convolution_divide_fusion = f32[64,256]{1,0:T(8,128)} fusion(f32[4096,256]{1,0:T(8,128)} %bitcast.43, s32[4096]{0:T(1024)S(1)} %eq.34, f32[64]{0:T(128)S(1)} %add_sqrt_fusion), kind=kOutput, calls=%fused_computation.75 | convolution fusion | flops 805584896 | bytes 4276480 | tf_op jit(solution)/shard_map/dot_general | solution.py:107
  (64 shorter events, 8.2 us)
Async XLA Ops:
  1.4 1.5 copy-start.1
  1.4 1.7 copy-start
  3.0 68.7 %collective-permute-start = (bf16[16,2,2048]{2,0,1:T(8,128)(2,1)S(1)}, bf16[16,2,2048]{2,0,1:T(8,128)(2,1)S(1)}, u32[]{:S(2)}, u32[]{:S(2)}) collective-permute-start(bf16[16,2,2048]{2,0,1:T(8,128)(2,1)S(1)} %get-tuple-element.8), channel_id=1, source_target_pairs={{0,1},{1,2},{2,3},{3,4},{4,5},{5,6},{6,7},{7,8},{8,9},{9,10},{10,1... | collective-permute-start | bytes 393224 | tf_op jit(solution)/shard_map/ppermute | solution.py:16
  50.4 99.7 %all-to-all-start = ((s32[128,1,32]{2,1,0:T(1,128)}), s32[128,1,32]{2,1,0:T(1,128)S(1)}, u32[]{:S(2)}, u32[]{:S(2)}) async-start(s32[128,1,32]{2,1,0:T(1,128)} %bitcast.4), calls=%async_computation | async-start | bytes 131072 | tf_op jit(solution)/shard_map/all_to_all | solution.py:96
  71.7 8.1 %collective-permute-start.1 = (bf16[16,2,2048]{2,0,1:T(8,128)(2,1)S(1)}, bf16[16,2,2048]{2,0,1:T(8,128)(2,1)S(1)}, u32[]{:S(2)}, u32[]{:S(2)}) collective-permute-start(bf16[16,2,2048]{2,0,1:T(8,128)(2,1)S(1)} %collective-permute-done), channel_id=1, source_target_pairs={{0,1},{1,2},{2,3},{3,4},{4,5},{5,6},{6,7},{7,8},{8,9},{9,10},{10,1... | collective-permute-start | bytes 393224 | tf_op jit(solution)/shard_map/ppermute | solution.py:16
  79.8 8.0 %collective-permute-start.2 = (bf16[16,2,2048]{2,0,1:T(8,128)(2,1)S(1)}, bf16[16,2,2048]{2,0,1:T(8,128)(2,1)S(1)}, u32[]{:S(2)}, u32[]{:S(2)}) collective-permute-start(bf16[16,2,2048]{2,0,1:T(8,128)(2,1)S(1)} %collective-permute-done.1), channel_id=1, source_target_pairs={{0,1},{1,2},{2,3},{3,4},{4,5},{5,6},{6,7},{7,8},{8,9},{9,10},{10,1... | collective-permute-start | bytes 393224 | tf_op jit(solution)/shard_map/ppermute | solution.py:16
  87.8 8.0 %collective-permute-start.3 = (bf16[16,2,2048]{2,0,1:T(8,128)(2,1)S(1)}, bf16[16,2,2048]{2,0,1:T(8,128)(2,1)S(1)}, u32[]{:S(2)}, u32[]{:S(2)}) collective-permute-start(bf16[16,2,2048]{2,0,1:T(8,128)(2,1)S(1)} %collective-permute-done.2), channel_id=1, source_target_pairs={{0,1},{1,2},{2,3},{3,4},{4,5},{5,6},{6,7},{7,8},{8,9},{9,10},{10,1... | collective-permute-start | bytes 393224 | tf_op jit(solution)/shard_map/ppermute | solution.py:16
  95.8 8.0 %collective-permute-start.4 = (bf16[16,2,2048]{2,0,1:T(8,128)(2,1)S(1)}, bf16[16,2,2048]{2,0,1:T(8,128)(2,1)S(1)}, u32[]{:S(2)}, u32[]{:S(2)}) collective-permute-start(bf16[16,2,2048]{2,0,1:T(8,128)(2,1)S(1)} %collective-permute-done.3), channel_id=1, source_target_pairs={{0,1},{1,2},{2,3},{3,4},{4,5},{5,6},{6,7},{7,8},{8,9},{9,10},{10,1... | collective-permute-start | bytes 393224 | tf_op jit(solution)/shard_map/ppermute | solution.py:16
  103.8 8.0 %collective-permute-start.5 = (bf16[16,2,2048]{2,0,1:T(8,128)(2,1)S(1)}, bf16[16,2,2048]{2,0,1:T(8,128)(2,1)S(1)}, u32[]{:S(2)}, u32[]{:S(2)}) collective-permute-start(bf16[16,2,2048]{2,0,1:T(8,128)(2,1)S(1)} %collective-permute-done.4), channel_id=1, source_target_pairs={{0,1},{1,2},{2,3},{3,4},{4,5},{5,6},{6,7},{7,8},{8,9},{9,10},{10,1... | collective-permute-start | bytes 393224 | tf_op jit(solution)/shard_map/ppermute | solution.py:16
  111.8 8.0 %collective-permute-start.6 = (bf16[16,2,2048]{2,0,1:T(8,128)(2,1)S(1)}, bf16[16,2,2048]{2,0,1:T(8,128)(2,1)S(1)}, u32[]{:S(2)}, u32[]{:S(2)}) collective-permute-start(bf16[16,2,2048]{2,0,1:T(8,128)(2,1)S(1)} %collective-permute-done.5), channel_id=1, source_target_pairs={{0,1},{1,2},{2,3},{3,4},{4,5},{5,6},{6,7},{7,8},{8,9},{9,10},{10,1... | collective-permute-start | bytes 393224 | tf_op jit(solution)/shard_map/ppermute | solution.py:16
  119.8 8.0 %collective-permute-start.7 = (bf16[16,2,2048]{2,0,1:T(8,128)(2,1)S(1)}, bf16[16,2,2048]{2,0,1:T(8,128)(2,1)S(1)}, u32[]{:S(2)}, u32[]{:S(2)}) collective-permute-start(bf16[16,2,2048]{2,0,1:T(8,128)(2,1)S(1)} %collective-permute-done.6), channel_id=1, source_target_pairs={{0,1},{1,2},{2,3},{3,4},{4,5},{5,6},{6,7},{7,8},{8,9},{9,10},{10,1... | collective-permute-start | bytes 393224 | tf_op jit(solution)/shard_map/ppermute | solution.py:16
  150.1 59.4 %all-to-all-start.1 = ((f32[128,32,256]{2,1,0:T(8,128)}), f32[128,32,256]{2,1,0:T(8,128)}, u32[]{:S(2)}, u32[]{:S(2)}) async-start(f32[128,32,256]{2,1,0:T(8,128)} %bitcast.77), calls=%async_computation.1 | async-start | bytes 8388608 | tf_op jit(solution)/shard_map/all_to_all | solution.py:89
where the time goes:
time: 215 us; the launch traced here: 214 us
  waiting for transfers between devices  106 us (49%)
  local copies, waits for them, and re-layouts  54.2 us (25%)
  other arithmetic  22.5 us (10%)
  starting transfers between devices  19.8 us (9%)
  matrix products  10.3 us (5%)
    ppermute x8, waiting for transfers between devices, from_behind(): return lax.ppermute(value, axis, pairs)  55.7 us
    all_to_all x1, waiting for transfers between devices, on_device(): lax.all_to_all(row_buffer.reshape(devices, capacity, LAGS), ('group', 'bl...  50.5 us
    gather x1, local copies, waits for them, and re-layouts, on_device(): rank_sorted = jnp.arange(row_count, dtype=jnp.int32) - starts[sorted_target]  12.6 us
    all_to_all x1, starting transfers between devices, on_device(): lax.all_to_all(bin_buffer.reshape(devices, capacity), ('group', 'blk'), s...  12.5 us
    gather x1, local copies, waits for them, and re-layouts, on_device(): sorted_target = target[sort_order]  11.8 us
    scatter x1, local copies, waits for them, and re-layouts, on_device(): jnp.zeros((devices * capacity, LAGS), jnp.float32).at[slot_index]  11.2 us
    cos x1, other arithmetic, build_table(): jnp.cos(angles)  8.24 us
    scatter x1, local copies, waits for them, and re-layouts, on_device(): jnp.full((devices * capacity,), -1, jnp.int32).at[slot_index].set(bin_list)  8.23 us
  transfers between devices with their start and end apart: 10, of which 8 were waited for; matrix products, arithmetic and copies ran while one was open for 37% of the time, Pallas kernels for 0%

commit v1 on v0

v1 whole, which is shorter than its diff:
```python
import functools
import math

import jax
import jax.numpy as jnp
import numpy as np
from jax import lax
from jax.experimental import pallas as pl
from jax.experimental.pallas import tpu as pltpu
from jax.sharding import PartitionSpec as P

CH = 16
FREQS = 2048
LAGS = 256
BINS_DEV = 64
MESH = pl.DeviceIdType.MESH
BF = jnp.bfloat16
F32 = jnp.float32

S_SIB, S_FLIP, S_Z, S_RELAY, S_ROWS, S_CODE, S_A, S_B = 0, 1, 1, 5, 8, 13, 14, 30
N_SEM = S_B + 64


def table_constant(width, lag_count):
    frequency = np.arange(width, dtype=np.int32)
    lag_offset = np.arange(lag_count, dtype=np.int32) - lag_count // 2
    product = frequency[:, None] * lag_offset[None, :] % (2 * width)
    angles = product.astype(np.float32) * np.float32(math.pi / width)
    norm = np.float32(1.0 / math.sqrt(width))
    whole = np.concatenate([np.cos(angles), -np.sin(angles)], axis=0) * norm
    return whole.astype(jnp.bfloat16)


def place(x, y, z, core):
    return (x * 2 + lax.rem(y, 2), lax.div(y, 2) * 8 + z * 2 + core)


def kernel(spec_ref, live_ref, code_ref, table_hbm, out_ref, own, spread, blocks, table, cross,
           rows, codes, own_sum, dense, got_a, part, got_b, send_sem, recv_sem, table_sem):
    group, blk = lax.axis_index("group"), lax.axis_index("blk")
    mx, core = lax.div(group, 2), lax.rem(blk, 2)
    my = lax.div(blk, 8) * 2 + lax.rem(group, 2)
    mz = lax.rem(lax.div(blk, 2), 4)

    def at(dx, dy, dz):
        return place(lax.rem(mx + dx, 4), lax.rem(my + dy, 4), lax.rem(mz + dz, 4), core)

    sibling = place(mx, my, mz, 1 - core)

    def send(src, dst, number, device):
        return pltpu.make_async_remote_copy(
            src_ref=src, dst_ref=dst, send_sem=send_sem.at[number], recv_sem=recv_sem.at[number],
            device_id=device, device_id_type=MESH)

    barrier = pltpu.get_barrier_semaphore()
    near = [(dx, dy, dz) for dx in range(4) for dy in range(4) for dz in range(4)
            if 0 < (dx > 0) + (dy > 0) + (dz > 0) < 3]
    pl.semaphore_signal(barrier, inc=1, device_id=sibling, device_id_type=MESH)
    for offset in near:
        pl.semaphore_signal(barrier, inc=1, device_id=at(*offset), device_id_type=MESH)

    table_copy = pltpu.make_async_copy(table_hbm, table, table_sem)
    table_copy.start()

    values = spec_ref[...].astype(F32)
    real, imag = values[:, 0, :], values[:, 1, :]
    energy = real * real + imag * imag
    lane = lax.broadcasted_iota(jnp.int32, energy.shape, 1)
    smooth = energy
    for bit in (1, 2, 4):
        other = jnp.where((lane & bit) == 0, pltpu.roll(smooth, FREQS - bit, 1),
                          pltpu.roll(smooth, bit, 1))
        smooth = smooth + other
    smooth = smooth * 0.125
    level = jnp.sum(energy, axis=1, keepdims=True) * (1.0 / FREQS)
    row = lax.broadcasted_iota(jnp.int32, (CH, 1), 0)
    alive = jnp.where(row < live_ref[0], 1.0, 0.0).astype(F32)
    inverse = lax.rsqrt(smooth + 0.1 * level + 1e-06) * alive
    own[0] = (real * inverse).astype(BF)
    own[1] = (imag * inverse).astype(BF)

    pl.semaphore_wait(barrier, len(near) + 1)

    sib_copy = send(own, blocks.at[0, core], S_SIB, sibling)
    flip_copy = send(own, blocks.at[4, core], S_FLIP, at(0, 2, 0))
    code_copy = send(code_ref, codes, S_CODE, sibling)
    sib_copy.start()
    flip_copy.start()
    code_copy.start()
    blocks[0, core] = own[...]

    z_copies = [None]
    for k in range(1, 4):
        source = lax.div(mz + k, 4) * 4
        z_copies.append(send(blocks.at[source, core], blocks.at[k, core], S_Z + k, at(0, 0, k)))
    for k in range(1, 4):
        @pl.when(mz + k < 4)
        def _(k=k):
            z_copies[k].start()
    flip_copy.wait_recv()
    for k in range(1, 4):
        @pl.when(mz + k >= 4)
        def _(k=k):
            z_copies[k].start()

    def relay(k):
        return send(blocks.at[k, core], blocks.at[k, core], S_RELAY + k - 1, sibling)

    relay(4).start()

    for part_of in range(2):
        for i in range(CH):
            spread[part_of, i] = jnp.broadcast_to(own[part_of, i:i + 1, :], (CH, FREQS))

    def form(place_in, k, far_core):
        def columns(c, carry):
            cols = pl.ds(pl.multiple_of(c * 256, 256), 256)
            cols_imag = pl.ds(pl.multiple_of(c * 256 + FREQS, 256), 256)
            far_r = blocks[k, far_core, 0, :, cols]
            far_i = blocks[k, far_core, 1, :, cols]
            for i in range(CH):
                near_r = spread[0, i, :, cols]
                near_i = spread[1, i, :, cols]
                here = pl.ds(place_in * 256 + i * CH, CH)
                cross[here, cols] = near_r * far_r + near_i * far_i
                cross[here, cols_imag] = near_i * far_r - near_r * far_i
            return carry
        lax.fori_loop(0, FREQS // 256, columns, 0)

    row_copies = []
    sib_copy.wait_recv()
    for k in range(1, 5):
        if k < 4:
            z_copies[k].wait_recv()
            relay(k).start()
        relay(k).wait_recv()
        form(0, k - core, 1 - core)
        form(1, k, core)
        if k == 1:
            table_copy.wait()
        here = pl.ds((k - 1) * 512, 512)
        rows[0, here] = jnp.dot(cross[...], table[...], preferred_element_type=F32).astype(BF)
        copy = send(rows.at[0, here], rows.at[1, here], S_ROWS + k, sibling)
        copy.start()
        row_copies.append(copy)

    code_copy.wait_recv()

    def place_of(code):
        owner, slot = code // 64, code % 64
        ox, oz, oc = owner // 32, owner // 2 % 4, owner % 2
        oy = owner // 8 % 2 * 2 + owner // 16 % 2
        dx, dy, dz = (ox - mx + 4) % 4, (oy - my + 4) % 4, (oz - mz + 4) % 4
        kind = slot // 16
        axis = jnp.where(kind == 3, core, kind)
        along = jnp.where(axis == 0, dx, jnp.where(axis == 1, dy, dz))
        first = jnp.where(axis == 0, dy, dx)
        second = jnp.where(axis == 2, dy, dz)
        spot = (kind * 4 + along) * 256 + (first * 4 + second) * 16 + slot % 16
        return jnp.where(oc == core, spot, -1)

    spots = [place_of(code_ref[...]), place_of(codes[...])]

    for copy in row_copies:
        copy.wait_recv()

    def axis_of(kind):
        axis = kind - lax.div(kind, 3) * (3 - core)
        ex, ez = lax.div(2 - axis, 2), lax.div(axis, 2)
        return ex, 1 - ex - ez, ez

    def copy_a(kind, along):
        ex, ey, ez = axis_of(kind)
        number = kind * 4 + along
        return send(dense.at[number], got_a.at[number], S_A + number,
                    at(ex * along, ey * along, ez * along))

    def tile_sum(number):
        sub = lax.broadcasted_iota(jnp.int32, (256, 2048), 0) + number * 256
        total = None
        for half in range(2):
            hot = jnp.where(sub == spots[half], 1.0, 0.0).astype(BF)
            term = jnp.dot(hot, rows[half], preferred_element_type=F32)
            total = term if total is None else total + term
        return total

    def tile(step, carry):
        along, kind = 3 - lax.div(step, 4), lax.rem(step, 4)
        number = kind * 4 + along
        dense[number] = tile_sum(number).astype(BF)
        copy_a(kind, along).start()
        return carry

    lax.fori_loop(0, 12, tile, 0)

    def tile_own(kind, carry):
        own_sum[kind] = tile_sum(kind * 4)
        return carry

    lax.fori_loop(0, 4, tile_own, 0)

    def copy_b(kind, spot):
        ex, ey, ez = axis_of(kind)
        first, second = lax.div(spot, 4), lax.rem(spot, 4)
        dx = (1 - ex) * first
        dy = ex * first + ez * second
        dz = (1 - ez) * second
        return send(part.at[kind, spot], got_b.at[kind, spot], S_B + kind * 16 + spot,
                    at(dx, dy, dz))

    def finish_a(kind, carry):
        total = own_sum[kind]
        for along in range(1, 4):
            copy_a(kind, along).wait_recv()
            total = total + got_a[kind * 4 + along].astype(F32)
        part[kind] = total.astype(BF).reshape(16, 16, LAGS)

        def go(spot, inner):
            copy_b(kind, spot).start()
            return inner
        lax.fori_loop(1, 16, go, 0)
        return carry

    lax.fori_loop(0, 4, finish_a, 0)

    def finish_b(kind, carry):
        def take(spot, total):
            copy_b(kind, spot).wait_recv()
            return total + got_b[kind, spot].astype(F32)
        total = lax.fori_loop(1, 16, take, part[kind, 0].astype(F32))
        out_ref[pl.ds(pl.multiple_of(kind * 16, 16), 16), :] = total
        return carry

    lax.fori_loop(0, 4, finish_b, 0)

    sib_copy.wait_send()
    flip_copy.wait_send()
    code_copy.wait_send()
    for k in range(1, 4):
        z_copies[k].wait_send()
    for k in range(1, 5):
        relay(k).wait_send()
        row_copies[k - 1].wait_send()

    def sent_a(step, carry):
        copy_a(lax.rem(step, 4), 3 - lax.div(step, 4)).wait_send()
        return carry
    lax.fori_loop(0, 12, sent_a, 0)

    def sent_b(step, carry):
        copy_b(lax.div(step, 15), lax.rem(step, 15) + 1).wait_send()
        return carry
    lax.fori_loop(0, 60, sent_b, 0)


def stack_sums(spectra, live_count, code, table):
    vmem = pl.BlockSpec(memory_space=pltpu.VMEM)
    return pl.pallas_call(
        kernel,
        out_shape=jax.ShapeDtypeStruct((BINS_DEV, LAGS), F32),
        in_specs=[vmem, pl.BlockSpec(memory_space=pltpu.SMEM), vmem,
                  pl.BlockSpec(memory_space=pl.ANY)],
        out_specs=vmem,
        scratch_shapes=[
            pltpu.VMEM((2, CH, FREQS), BF),
            pltpu.VMEM((2, CH, CH, FREQS), BF),
            pltpu.VMEM((5, 2, 2, CH, FREQS), BF),
            pltpu.VMEM((2 * FREQS, LAGS), BF),
            pltpu.VMEM((512, 2 * FREQS), BF),
            pltpu.VMEM((2, 2048, LAGS), BF),
            pltpu.VMEM((1, 2048), jnp.int32),
            pltpu.VMEM((4, 256, LAGS), F32),
            pltpu.VMEM((16, 256, LAGS), BF),
            pltpu.VMEM((16, 256, LAGS), BF),
            pltpu.VMEM((4, 16, 16, LAGS), BF),
            pltpu.VMEM((4, 16, 16, LAGS), BF),
            pltpu.SemaphoreType.DMA((N_SEM,)),
            pltpu.SemaphoreType.DMA((N_SEM,)),
            pltpu.SemaphoreType.DMA,
        ],
        compiler_params=pltpu.CompilerParams(
            collective_id=0, has_side_effects=True, vmem_limit_bytes=56 * 1024 * 1024),
        cost_estimate=pl.CostEstimate(
            flops=13_000_000_000, bytes_accessed=4_000_000, transcendentals=40_000),
    )(spectra, live_count, code, table)


def on_device(spectra, live_count, owner_list, bin_list):
    owner = owner_list[:, 0]
    code = (owner * BINS_DEV + bin_list).reshape(1, -1)
    named = (jnp.arange(128, dtype=jnp.int32)[:, None] == owner[None, :]).astype(BF)
    binned = (jnp.arange(BINS_DEV, dtype=jnp.int32)[:, None] == bin_list[None, :]).astype(BF)
    hits = lax.dot_general(named, binned, (((1,), (1,)), ((), ())), preferred_element_type=F32)
    counts = lax.psum_scatter(hits, ("group", "blk"), scatter_dimension=0, tiled=True)
    table = jnp.asarray(table_constant(FREQS, LAGS))
    sums = stack_sums(spectra, live_count, code, table)
    return sums / jnp.sqrt(counts.reshape(BINS_DEV, 1) + 1.0)


def solution(mesh):
    return jax.shard_map(
        on_device,
        mesh=mesh,
        in_specs=(
            P(("group", "blk"), None, None),
            P(("group", "blk")),
            P(("group", "blk"), None),
            P(("group", "blk")),
        ),
        out_specs=P(("group", "blk"), None),
        check_vma=False,
    )
```

time: 215 us -> 132 us (0.61)
  waiting for transfers between devices: 106 us -> 0 us
  blocking collectives: 0 us -> 68.4 us
  Pallas kernels: 0 us -> 58.4 us
  local copies, waits for them, and re-layouts: 54.2 us -> 0 us
  starting transfers between devices: 19.8 us -> 0 us
  other arithmetic: 22.5 us -> 2.88 us
  matrix products: 10.3 us -> 1.05 us
    unnamed x0 -> x1, blocking collectives: none -> 68.4 us
    pallas_call x0 -> x1, Pallas kernels: none -> 58.4 us  [stack_sums(): pl.pallas_call(kernel, out_shape=jax.ShapeDtypeStruct((BINS_DEV, LAGS), F...]
    ppermute x8 -> x0, waiting for transfers between devices: 55.7 us -> none  [from_behind(): return lax.ppermute(value, axis, pairs)]
    all_to_all x2 -> x0, waiting for transfers between devices: 50.5 us -> none  [the longest x1 50.5 us: on_device(): lax.all_to_all(row_buffer.reshape(devices, capacity, LAGS), ('group', 'bl...]
    scatter x3 -> x0, local copies, waits for them, and re-layouts: 27.5 us -> none  [the longest x1 11.2 us: on_device(): jnp.zeros((devices * capacity, LAGS), jnp.float32).at[slot_index]]
    gather x2 -> x0, local copies, waits for them, and re-layouts: 24.4 us -> none  [the longest x1 12.6 us: on_device(): rank_sorted = jnp.arange(row_count, dtype=jnp.int32) - starts[sorted_target]]
    all_to_all x2 -> x0, starting transfers between devices: 19.7 us -> none  [the longest x1 12.5 us: on_device(): lax.all_to_all(bin_buffer.reshape(devices, capacity), ('group', 'blk'), s...]
    dot_general x9 -> x1, matrix products: 10.3 us -> 1.05 us  [on_device(): lax.dot_general(named, binned, (((1,), (1,)), ((), ())), preferred_elemen...]
  transfers between devices with their start and end apart: 10 -> 0, of which waited for: 8 -> 0; matrix products, arithmetic and copies ran while one was open for 37% -> 0% of each run, Pallas kernels for 0% -> 0%
where the time goes in v1:
time: 132 us; the launch traced here: 131 us
  blocking collectives  68.4 us (52%)
  Pallas kernels  58.4 us (44%)
  other arithmetic  2.88 us (2%)
    unnamed x1, blocking collectives  68.4 us
    pallas_call x1, Pallas kernels, stack_sums(): pl.pallas_call(kernel, out_shape=jax.ShapeDtypeStruct((BINS_DEV, LAGS), F...  58.4 us

profile of v1, /device:TPU:0, one launch (start us, length us, event | category | flops | bytes accessed | tf_op | source)
XLA Modules:
  0.0 131.4 jit_solution(13813740062108229591)
XLA Ops:
  0.0 1.0 fusion
  1.1 68.4 %all-reduce = f32[128,64]{1,0:T(8,128)S(1)} all-reduce(f32[128,64]{1,0:T(8,128)S(1)} %fusion), channel_id=2, replica_groups=mesh['group'=8,'blk'=16] {'group','blk'}, use_global_device_ids=true, to_apply=%region_0.0.clone | all-reduce | flops 8192 | bytes 65536
  69.5 1.3 %multiply_add_fusion = s32[2048]{0:T(1024)} fusion(s32[2048]{0:T(1024)} %param.8, s32[2048]{0:T(1024)} %bitcast.5), kind=kLoop, calls=%fused_computation.6 | loop fusion | flops 4096 | bytes 24576 | tf_op jit(solution)/shard_map/add | solution.py:290
  71.5 58.4 %shard_map.55 = f32[64,256]{1,0:T(8,128)} custom-call(bf16[16,2,2048]{2,1,0:T(2,128)(2,1)} %spec_ref.1, s32[1]{0:T(128)S(6)} %copy.6.live_ref, s32[1,2048]{1,0:T(1,128)} %bitcast.6, bf16[4096,256]{1,0:T(8,128)(2,1)} %constant.6.clone.table_hbm), custom_call_target="tpu_custom_call" | custom-call | flops 12999999488 | bytes 4000000 | tf_op jit(solution)/shard_map/pallas_call | solution.py:258
  129.9 1.6 %broadcast_divide_fusion = f32[64,256]{1,0:T(8,128)} fusion(f32[64,256]{1,0:T(8,128)} %shard_map.55, f32[64]{0:T(128)S(1)} %fusion.4), kind=kLoop, calls=%fused_computation.5 | loop fusion | flops 16384 | bytes 131328 | tf_op jit(solution)/shard_map/div | solution.py:297
  (1 shorter events, 0.0 us)

commit v2 on v1

v2 whole, which is shorter than its diff:
```python
import functools
import math

import jax
import jax.numpy as jnp
import numpy as np
from jax import lax
from jax.experimental import pallas as pl
from jax.experimental.pallas import tpu as pltpu
from jax.sharding import PartitionSpec as P

CH = 16
FREQS = 2048
LAGS = 256
BINS_DEV = 64
MESH = pl.DeviceIdType.MESH
BF = jnp.bfloat16
F32 = jnp.float32

S_SIB, S_FLIP, S_Z, S_RELAY, S_ROWS, S_CODE, S_N, S_A, S_B = 0, 2, 4, 12, 20, 28, 29, 38, 54
N_SEM = S_B + 4
ORDER = (4, 1, 3, 2)


def table_constant(width, lag_count):
    frequency = np.arange(width, dtype=np.int32)
    lag_offset = np.arange(lag_count, dtype=np.int32) - lag_count // 2
    product = frequency[:, None] * lag_offset[None, :] % (2 * width)
    angles = product.astype(np.float32) * np.float32(math.pi / width)
    norm = np.float32(1.0 / math.sqrt(width))
    whole = np.concatenate([np.cos(angles), -np.sin(angles)], axis=0) * norm
    return whole.astype(jnp.bfloat16)


def place(x, y, z, core):
    return (x * 2 + lax.rem(y, 2), lax.div(y, 2) * 8 + z * 2 + core)


def kernel(spec_ref, live_ref, owner_ref, bin_ref, table_hbm, out_ref, own, spread, blocks, table,
           cross, rows, codes, own_sum, dense, got_a, part, got_b, tally, got_n,
           send_sem, recv_sem, table_sem):
    group, blk = lax.axis_index("group"), lax.axis_index("blk")
    mx, core = lax.div(group, 2), lax.rem(blk, 2)
    my = lax.div(blk, 8) * 2 + lax.rem(group, 2)
    mz = lax.rem(lax.div(blk, 2), 4)

    def at(dx, dy, dz):
        return place(lax.rem(mx + dx, 4), lax.rem(my + dy, 4), lax.rem(mz + dz, 4), core)

    sibling = place(mx, my, mz, 1 - core)

    def send(src, dst, number, device):
        return pltpu.make_async_remote_copy(
            src_ref=src, dst_ref=dst, send_sem=send_sem.at[number], recv_sem=recv_sem.at[number],
            device_id=device, device_id_type=MESH)

    barrier = pltpu.get_barrier_semaphore()
    pl.semaphore_signal(barrier, inc=1, device_id=sibling, device_id_type=MESH)
    for v in range(1, 4):
        for device in (at(0, 0, v), at(0, v, 0), at(v, 0, 0)):
            pl.semaphore_signal(barrier, inc=1, device_id=device, device_id_type=MESH)

    table_copy = pltpu.make_async_copy(table_hbm, table, table_sem)
    table_copy.start()

    values = spec_ref[...].astype(F32)
    real, imag = values[:, 0, :], values[:, 1, :]
    energy = real * real + imag * imag
    lane = lax.broadcasted_iota(jnp.int32, energy.shape, 1)
    smooth = energy
    for bit in (1, 2, 4):
        other = jnp.where((lane & bit) == 0, pltpu.roll(smooth, FREQS - bit, 1),
                          pltpu.roll(smooth, bit, 1))
        smooth = smooth + other
    smooth = smooth * 0.125
    level = jnp.sum(energy, axis=1, keepdims=True) * (1.0 / FREQS)
    row = lax.broadcasted_iota(jnp.int32, (CH, 1), 0)
    alive = jnp.where(row < live_ref[0], 1.0, 0.0).astype(F32)
    inverse = lax.rsqrt(smooth + 0.1 * level + 1e-06) * alive
    own[0] = (real * inverse).astype(BF)
    own[1] = (imag * inverse).astype(BF)
    codes[0] = owner_ref[...] * BINS_DEV + bin_ref[...]
    blocks[0, core] = own[...]

    for part_of in range(2):
        for i in range(CH):
            spread[part_of, i] = jnp.broadcast_to(own[part_of, i:i + 1, :], (CH, FREQS))

    pl.semaphore_wait(barrier, 10)

    def flip(half):
        return send(own.at[half], blocks.at[4, core, half], S_FLIP + half, at(0, 2, 0))

    def along_z(k, half):
        source = lax.div(mz + k, 4) * 4
        return send(blocks.at[source, core, half], blocks.at[k, core, half],
                    S_Z + 2 * k + half - 2, at(0, 0, k))

    def relay(k, half):
        return send(blocks.at[k, core, half], blocks.at[k, core, half],
                    S_RELAY + 2 * k + half - 2, sibling)

    def first_relay(half):
        spot = core * 4
        return send(blocks.at[spot, core, half], blocks.at[spot, core, half], S_SIB + half, sibling)

    code_copy = send(codes.at[0], codes.at[1], S_CODE, sibling)
    code_copy.start()
    for half in range(2):
        flip(half).start()

    @pl.when(core == 0)
    def _():
        for half in range(2):
            first_relay(half).start()

    for half in range(2):
        for k in ORDER[1:]:
            @pl.when(mz + k < 4)
            def _(k=k, half=half):
                along_z(k, half).start()

    def offsets_of(code):
        owner = code // 64
        ox, oz, oc = owner // 32, owner // 2 % 4, owner % 2
        oy = owner // 8 % 2 * 2 + owner // 16 % 2
        return (ox - mx + 4) % 4, (oy - my + 4) % 4, (oz - mz + 4) % 4, oc

    def hits_of(code):
        dx, dy, dz, oc = offsets_of(code)
        whose = jnp.where(oc == core, dx * 32 + dy * 8 + dz, -1)
        down = lax.broadcasted_iota(jnp.int32, (128, 2048), 0)
        named = jnp.where(down == whose, 1.0, 0.0).astype(BF)
        binned = jnp.where(down == code % 64, 1.0, 0.0).astype(BF)
        return lax.dot_general(named, binned, (((1,), (1,)), ((), ())), preferred_element_type=F32)

    def copy_n(stage, v):
        spot = stage * 3 + v - 1
        if stage == 0:
            return send(tally.at[pl.ds(32 * v, 32)], got_n.at[spot], S_N + spot, at(v, 0, 0))
        if stage == 1:
            return send(tally.at[pl.ds(8 * v, 8)], got_n.at[spot, pl.ds(0, 8)], S_N + spot,
                        at(0, v, 0))
        return send(tally.at[pl.ds(0, 8)], got_n.at[spot, pl.ds(0, 8)], S_N + spot, at(0, 0, v))

    def tally_stage(stage):
        if stage > 0:
            rows_of = 32 if stage == 1 else 8
            total = tally[0:rows_of]
            for v in range(1, 4):
                copy_n(stage - 1, v).wait()
                total = total + got_n[(stage - 1) * 3 + v - 1, 0:rows_of]
            tally[0:rows_of] = total
        for v in range(1, 4):
            copy_n(stage, v).start()

    hits = hits_of(codes[0])

    for half in range(2):
        flip(half).wait_recv()
        for k in ORDER[1:]:
            @pl.when(mz + k >= 4)
            def _(k=k, half=half):
                along_z(k, half).start()

        @pl.when(core == 1)
        def _(half=half):
            first_relay(half).start()

    code_copy.wait_recv()
    tally[...] = hits + hits_of(codes[1])
    tally_stage(0)

    def form(place_in, k, far_core):
        far_r, far_i = blocks[k, far_core, 0], blocks[k, far_core, 1]
        for i in range(CH):
            near_r, near_i = spread[0, i], spread[1, i]
            here = pl.ds(place_in * 256 + i * CH, CH)
            cross[here, 0:FREQS] = near_r * far_r + near_i * far_i
            cross[here, FREQS:2 * FREQS] = near_i * far_r - near_r * far_i

    def row_copy(step):
        k = ORDER[step // 2]
        if step % 2:
            begin = (2 * k - 1) * 256
        else:
            far = k if k < 4 else 4 * (1 - core)
            begin = pl.multiple_of((2 * far - 2 + 2 * core) * 256, 256)
        here = pl.ds(begin, 256)
        return here, send(rows.at[0, here], rows.at[1, here], S_ROWS + step, sibling)

    def correlate(p):
        k = ORDER[p]
        form(1, k, core)
        if p == 0:
            for half in range(2):
                first_relay(half).wait_recv()
            table_copy.wait()
            form(0, 4 * (1 - core), 1 - core)
        else:
            for half in range(2):
                relay(k, half).wait_recv()
            form(0, k, 1 - core)
        made = jnp.dot(cross[...], table[...], preferred_element_type=F32).astype(BF)
        for side in range(2):
            here, copy = row_copy(2 * p + side)
            rows[0, here] = made[side * 256:(side + 1) * 256]
            copy.start()

    def arrive(k):
        for half in range(2):
            along_z(k, half).wait_recv()
            relay(k, half).start()

    correlate(0)
    arrive(1)
    tally_stage(1)
    arrive(3)
    correlate(1)
    arrive(2)
    tally_stage(2)
    correlate(2)

    def place_of(code):
        slot = code % 64
        dx, dy, dz, oc = offsets_of(code)
        kind = slot // 16
        axis = jnp.where(kind == 3, core, kind)
        along = jnp.where(axis == 0, dx, jnp.where(axis == 1, dy, dz))
        first = jnp.where(axis == 0, dy, dx)
        second = jnp.where(axis == 2, dy, dz)
        spot = (along * 4 + kind) * 256 + (first * 4 + second) * 16 + slot % 16
        return jnp.where(oc == core, spot, -1)

    code_copy.wait_send()
    codes[0] = place_of(codes[0])
    codes[1] = place_of(codes[1])

    correlate(3)

    def axis_of(kind):
        axis = kind - lax.div(kind, 3) * (3 - core)
        ex, ez = lax.div(2 - axis, 2), lax.div(axis, 2)
        return ex, 1 - ex - ez, ez

    def copy_a(kind, along):
        ex, ey, ez = axis_of(kind)
        here = pl.ds(pl.multiple_of(kind * 256, 256), 256)
        return send(dense.at[along, here], got_a.at[along, here], S_A + along * 4 + kind,
                    at(ex * along, ey * along, ez * along))

    def group_half(along, half):
        down = lax.broadcasted_iota(jnp.int32, (1024, 2048), 0)
        hot = jnp.where(down == codes[half] - along * 1024, 1.0, 0.0).astype(BF)
        return jnp.dot(hot, rows[half], preferred_element_type=F32)

    own_sum[...] = group_half(2, 0)
    for step in range(8):
        row_copy(step)[1].wait_recv()

    def send_group(along):
        for kind in range(4):
            copy_a(kind, along).start()

    dense[2] = (own_sum[...] + group_half(2, 1)).astype(BF)
    send_group(2)
    for along in (1, 3):
        dense[along] = (group_half(along, 0) + group_half(along, 1)).astype(BF)
        send_group(along)
    own_sum[...] = group_half(0, 0) + group_half(0, 1)

    def copy_b(kind, spot):
        ex, ey, ez = axis_of(kind)
        first, second = lax.div(spot, 4), lax.rem(spot, 4)
        dx = (1 - ex) * first
        dy = ex * first + ez * second
        dz = (1 - ez) * second
        return send(part.at[kind, spot], got_b.at[kind, spot], S_B + kind, at(dx, dy, dz))

    def all_b(kind):
        rest = pl.ds(1, 15)
        return send(part.at[kind, rest], got_b.at[kind, rest], S_B + kind, sibling)

    for kind in range(4):
        here = pl.ds(kind * 256, 256)
        total = own_sum[here]
        for along in (2, 1, 3):
            copy_a(kind, along).wait_recv()
            total = total + got_a[along, here].astype(F32)
        part[kind] = total.astype(BF).reshape(16, 16, LAGS)

        def go(spot, carry, kind=kind):
            copy_b(kind, spot).start()
            return carry
        lax.fori_loop(1, 16, go, 0)

    count = tally[0:1]
    for v in range(1, 4):
        copy_n(2, v).wait()
        count = count + got_n[5 + v, v:v + 1]
    shape = (BINS_DEV, 128)
    diagonal = lax.broadcasted_iota(jnp.int32, shape, 0) == lax.broadcasted_iota(jnp.int32, shape, 1)
    count = jnp.sum(jnp.where(diagonal, count, 0.0), axis=1, keepdims=True)
    scale = lax.rsqrt(count + 1.0)

    for half in range(2):
        flip(half).wait_send()
        first_relay(half).wait_send()
        for k in range(1, 4):
            relay(k, half).wait_send()
            along_z(k, half).wait_send()
    for step in range(8):
        row_copy(step)[1].wait_send()
    for along in range(1, 4):
        for kind in range(4):
            copy_a(kind, along).wait_send()

    for kind in range(4):
        all_b(kind).wait_recv()
        total = part[kind, 0].astype(F32)
        for spot in range(1, 16):
            total = total + got_b[kind, spot].astype(F32)
        out_ref[kind * 16:(kind + 1) * 16, :] = total * scale[kind * 16:(kind + 1) * 16]

    for kind in range(4):
        all_b(kind).wait_send()


def stacks(spectra, live_count, owner, slot, table):
    vmem = pl.BlockSpec(memory_space=pltpu.VMEM)
    return pl.pallas_call(
        kernel,
        out_shape=jax.ShapeDtypeStruct((BINS_DEV, LAGS), F32),
        in_specs=[vmem, pl.BlockSpec(memory_space=pltpu.SMEM), vmem, vmem,
                  pl.BlockSpec(memory_space=pl.ANY)],
        out_specs=vmem,
        scratch_shapes=[
            pltpu.VMEM((2, CH, FREQS), BF),
            pltpu.VMEM((2, CH, CH, FREQS), BF),
            pltpu.VMEM((5, 2, 2, CH, FREQS), BF),
            pltpu.VMEM((2 * FREQS, LAGS), BF),
            pltpu.VMEM((512, 2 * FREQS), BF),
            pltpu.VMEM((2, 2048, LAGS), BF),
            pltpu.VMEM((2, 1, 2048), jnp.int32),
            pltpu.VMEM((1024, LAGS), F32),
            pltpu.VMEM((4, 1024, LAGS), BF),
            pltpu.VMEM((4, 1024, LAGS), BF),
            pltpu.VMEM((4, 16, 16, LAGS), BF),
            pltpu.VMEM((4, 16, 16, LAGS), BF),
            pltpu.VMEM((128, 128), F32),
            pltpu.VMEM((9, 32, 128), F32),
            pltpu.SemaphoreType.DMA((N_SEM,)),
            pltpu.SemaphoreType.DMA((N_SEM,)),
            pltpu.SemaphoreType.DMA,
        ],
        compiler_params=pltpu.CompilerParams(
            collective_id=0, has_side_effects=True, vmem_limit_bytes=56 * 1024 * 1024),
        cost_estimate=pl.CostEstimate(
            flops=13_000_000_000, bytes_accessed=4_000_000, transcendentals=40_000),
    )(spectra, live_count, owner, slot, table)


def on_device(spectra, live_count, owner_list, bin_list):
    table = jnp.asarray(table_constant(FREQS, LAGS))
    return stacks(spectra, live_count, owner_list.reshape(1, -1), bin_list.reshape(1, -1), table)


def solution(mesh):
    return jax.shard_map(
        on_device,
        mesh=mesh,
        in_specs=(
            P(("group", "blk"), None, None),
            P(("group", "blk")),
            P(("group", "blk"), None),
            P(("group", "blk")),
        ),
        out_specs=P(("group", "blk"), None),
        check_vma=False,
    )
```

time: 132 us -> 57.3 us (0.43)
  blocking collectives: 68.4 us -> 0 us
  Pallas kernels: 58.4 us -> 55 us
  other arithmetic: 2.88 us -> 0 us
  local copies, waits for them, and re-layouts: 0 us -> 1.47 us
    unnamed x1 -> x0, blocking collectives: 68.4 us -> none
    pallas_call x1, Pallas kernels: 58.4 us -> 55 us  [stacks(): pl.pallas_call(kernel, out_shape=jax.ShapeDtypeStruct((BINS_DEV, LAGS), F...]
    div x1 -> x0, other arithmetic: 1.55 us -> none  [on_device(): return sums / jnp.sqrt(counts.reshape(BINS_DEV, 1) + 1.0)]
    unnamed x0 -> x1, local copies, waits for them, and re-layouts: none -> 1.47 us
where the time goes in v2:
time: 57.3 us; the launch traced here: 57.2 us
  Pallas kernels  55 us (96%)
  local copies, waits for them, and re-layouts  1.47 us (3%)
  between operations  0.66 us (1%)
    pallas_call x1, Pallas kernels, stacks(): pl.pallas_call(kernel, out_shape=jax.ShapeDtypeStruct((BINS_DEV, LAGS), F...  55 us
    unnamed x1, local copies, waits for them, and re-layouts  1.47 us

profile of v2, /device:TPU:0, one launch (start us, length us, event | category | flops | bytes accessed | tf_op | source)
XLA Modules:
  0.0 57.2 jit_solution(17713547151661870436)
XLA Ops:
  0.7 55.0 %shard_map.55 = f32[64,256]{1,0:T(8,128)} custom-call(bf16[16,2,2048]{2,1,0:T(2,128)(2,1)} %spec_ref.1, s32[1]{0:T(128)S(6)} %copy.7.live_ref, s32[1,2048]{1,0:T(1,128)} %bitcast.2, s32[1,2048]{1,0:T(1,128)} %bitcast.3, bf16[4096,256]{1,0:T(8,128)(2,1)} %constant.2.clone.table_hbm), custom_call_target="tpu_custom_call" | custom-call | flops 12999999488 | bytes 4000000 | tf_op jit(solution)/shard_map/pallas_call | solution.py:331
  55.7 1.5 %copy.8 = f32[64,256]{1,0:T(8,128)} copy(f32[64,256]{1,0:T(8,128)} %shard_map.55) | data formatting | bytes 131072

commit v3 on v2

--- a/solution.py
+++ b/solution.py
@@ -17,9 +17,10 @@
 BF = jnp.bfloat16
 F32 = jnp.float32
 
-S_SIB, S_FLIP, S_Z, S_RELAY, S_ROWS, S_CODE, S_N, S_A, S_B = 0, 2, 4, 12, 20, 28, 29, 38, 54
+S_SIB, S_FAR, S_CODE, S_ROWS, S_N, S_A, S_B = 0, 1, 7, 11, 15, 24, 40
 N_SEM = S_B + 4
-ORDER = (4, 1, 3, 2)
+OWN, BACK, OPPOSITE, FLIP = 0, 1, 2, 3
+HALF = FREQS // 2
 
 
 def table_constant(width, lag_count):
@@ -36,8 +37,8 @@
     return (x * 2 + lax.rem(y, 2), lax.div(y, 2) * 8 + z * 2 + core)
 
 
-def kernel(spec_ref, live_ref, owner_ref, bin_ref, table_hbm, out_ref, own, spread, blocks, table,
-           cross, rows, codes, own_sum, dense, got_a, part, got_b, tally, got_n,
+def kernel(spec_ref, live_ref, owner_ref, bin_ref, table_hbm, out_ref, own, blocks, table, cross,
+           codes, spots, mine, leaving, coming, rows, own_sum, dense, got_a, part, got_b, tally, got_n,
            send_sem, recv_sem, table_sem):
     group, blk = lax.axis_index("group"), lax.axis_index("blk")
     mx, core = lax.div(group, 2), lax.rem(blk, 2)
@@ -60,8 +61,12 @@
         for device in (at(0, 0, v), at(0, v, 0), at(v, 0, 0)):
             pl.semaphore_signal(barrier, inc=1, device_id=device, device_id_type=MESH)
 
-    table_copy = pltpu.make_async_copy(table_hbm, table, table_sem)
-    table_copy.start()
+    table_copies = []
+    for side in range(2):
+        here = pl.ds(pl.multiple_of(side * FREQS + core * HALF, HALF), HALF)
+        table_copies.append(pltpu.make_async_copy(
+            table_hbm.at[here], table.at[pl.ds(side * HALF, HALF)], table_sem.at[side]))
+        table_copies[side].start()
 
     values = spec_ref[...].astype(F32)
     real, imag = values[:, 0, :], values[:, 1, :]
@@ -77,48 +82,36 @@
     row = lax.broadcasted_iota(jnp.int32, (CH, 1), 0)
     alive = jnp.where(row < live_ref[0], 1.0, 0.0).astype(F32)
     inverse = lax.rsqrt(smooth + 0.1 * level + 1e-06) * alive
-    own[0] = (real * inverse).astype(BF)
-    own[1] = (imag * inverse).astype(BF)
-    codes[0] = owner_ref[...] * BINS_DEV + bin_ref[...]
-    blocks[0, core] = own[...]
-
-    for part_of in range(2):
-        for i in range(CH):
-            spread[part_of, i] = jnp.broadcast_to(own[part_of, i:i + 1, :], (CH, FREQS))
+    for side, values in enumerate((real, imag)):
+        white = (values * inverse).astype(BF)
+        for half in range(2):
+            own[half, side] = white[:, half * HALF:(half + 1) * HALF]
+    blocks[OWN, core] = own[core]
+    codes[OWN, core] = owner_ref[...] * BINS_DEV + bin_ref[...]
 
     pl.semaphore_wait(barrier, 10)
 
-    def flip(half):
-        return send(own.at[half], blocks.at[4, core, half], S_FLIP + half, at(0, 2, 0))
-
-    def along_z(k, half):
-        source = lax.div(mz + k, 4) * 4
-        return send(blocks.at[source, core, half], blocks.at[k, core, half],
-                    S_Z + 2 * k + half - 2, at(0, 0, k))
-
-    def relay(k, half):
-        return send(blocks.at[k, core, half], blocks.at[k, core, half],
-                    S_RELAY + 2 * k + half - 2, sibling)
-
-    def first_relay(half):
-        spot = core * 4
-        return send(blocks.at[spot, core, half], blocks.at[spot, core, half], S_SIB + half, sibling)
-
-    code_copy = send(codes.at[0], codes.at[1], S_CODE, sibling)
+    toward = {BACK: at(0, 0, 1), OPPOSITE: at(0, 0, 2), FLIP: at(0, 2, 0)}
+    sib_copy = send(own.at[1 - core], blocks.at[OWN, core], S_SIB, sibling)
+    sib_copy.start()
+    code_copy = send(codes.at[OWN, core], codes.at[OWN, core], S_CODE, sibling)
     code_copy.start()
-    for half in range(2):
-        flip(half).start()
-
-    @pl.when(core == 0)
-    def _():
-        for half in range(2):
-            first_relay(half).start()
-
-    for half in range(2):
-        for k in ORDER[1:]:
-            @pl.when(mz + k < 4)
-            def _(k=k, half=half):
-                along_z(k, half).start()
+
+    def far_copy(r, j):
+        q = core if j == 0 else 1 - core
+        return send(blocks.at[OWN, q], blocks.at[r, q], S_FAR + 2 * (r - 1) + j, toward[r])
+
+    def far_code(r):
+        return send(codes.at[OWN], codes.at[r], S_CODE + r, toward[r])
+
+    for r in (FLIP, BACK, OPPOSITE):
+        far_copy(r, 0).start()
+    sib_copy.wait_recv()
+    for r in (FLIP, BACK, OPPOSITE):
+        far_copy(r, 1).start()
+    code_copy.wait_recv()
+    for r in (FLIP, BACK, OPPOSITE):
+        far_code(r).start()
 
     def offsets_of(code):
         owner = code // 64
@@ -154,72 +147,78 @@
         for v in range(1, 4):
             copy_n(stage, v).start()
 
-    hits = hits_of(codes[0])
-
-    for half in range(2):
-        flip(half).wait_recv()
-        for k in ORDER[1:]:
-            @pl.when(mz + k >= 4)
-            def _(k=k, half=half):
-                along_z(k, half).start()
-
-        @pl.when(core == 1)
-        def _(half=half):
-            first_relay(half).start()
-
-    code_copy.wait_recv()
-    tally[...] = hits + hits_of(codes[1])
+    tally[...] = hits_of(codes[OWN, 0]) + hits_of(codes[OWN, 1])
     tally_stage(0)
 
-    def form(place_in, k, far_core):
-        far_r, far_i = blocks[k, far_core, 0], blocks[k, far_core, 1]
+    def pair_of(first, q, second, r, steps):
+        return first, q, second, r, steps + q - r
+
+    low = 1 - lax.div(mz + 3, 4)
+    high = lax.div(mz, 2)
+
+    def pick(flag, one, other):
+        return flag * one + (1 - flag) * other
+
+    near_first, near_second = pick(low, BACK, OWN), pick(low, OWN, BACK)
+    cross_first, cross_second = pick(low, FLIP, BACK), pick(low, BACK, FLIP)
+    far_first, far_second = pick(high, OWN, OPPOSITE), pick(high, OPPOSITE, OWN)
+    flip_first, flip_second = pick(high, OPPOSITE, FLIP), pick(high, FLIP, OPPOSITE)
+    pairs = [
+        [pair_of(OWN, 0, FLIP, 0, 8), pair_of(OWN, 0, FLIP, 1, 8),
+         pair_of(OWN, 1, FLIP, 1, 8), pair_of(OWN, 1, OWN, 0, 0)],
+        [pair_of(near_first, q, near_second, r, pick(low, 6, 2)) for q in (0, 1) for r in (0, 1)],
+        [pair_of(cross_first, q, cross_second, r, pick(low, 2, 6)) for q in (0, 1) for r in (0, 1)],
+        [pair_of(far_first, high, far_second, r, 4) for r in (0, 1)]
+        + [pair_of(flip_first, high, flip_second, r, 4) for r in (0, 1)],
+    ]
+
+    def form(slot, first, q, second, r):
+        far_r, far_i = blocks[second, r, 0], blocks[second, r, 1]
         for i in range(CH):
-            near_r, near_i = spread[0, i], spread[1, i]
-            here = pl.ds(place_in * 256 + i * CH, CH)
-            cross[here, 0:FREQS] = near_r * far_r + near_i * far_i
-            cross[here, FREQS:2 * FREQS] = near_i * far_r - near_r * far_i
-
-    def row_copy(step):
-        k = ORDER[step // 2]
-        if step % 2:
-            begin = (2 * k - 1) * 256
-        else:
-            far = k if k < 4 else 4 * (1 - core)
-            begin = pl.multiple_of((2 * far - 2 + 2 * core) * 256, 256)
-        here = pl.ds(begin, 256)
-        return here, send(rows.at[0, here], rows.at[1, here], S_ROWS + step, sibling)
+            near_r = jnp.broadcast_to(blocks[first, q, 0, i:i + 1, :], (CH, HALF))
+            near_i = jnp.broadcast_to(blocks[first, q, 1, i:i + 1, :], (CH, HALF))
+            here = pl.ds(slot * 256 + i * CH, CH)
+            cross[here, 0:HALF] = near_r * far_r + near_i * far_i
+            cross[here, HALF:FREQS] = near_i * far_r - near_r * far_i
+
+    def row_copy(p):
+        return send(leaving.at[p], coming.at[p], S_ROWS + p, sibling)
 
     def correlate(p):
-        k = ORDER[p]
-        form(1, k, core)
-        if p == 0:
-            for half in range(2):
-                first_relay(half).wait_recv()
-            table_copy.wait()
-            form(0, 4 * (1 - core), 1 - core)
-        else:
-            for half in range(2):
-                relay(k, half).wait_recv()
-            form(0, k, 1 - core)
-        made = jnp.dot(cross[...], table[...], preferred_element_type=F32).astype(BF)
-        for side in range(2):
-            here, copy = row_copy(2 * p + side)
-            rows[0, here] = made[side * 256:(side + 1) * 256]
-            copy.start()
-
-    def arrive(k):
-        for half in range(2):
-            along_z(k, half).wait_recv()
-            relay(k, half).start()
-
+        for slot, (first, q, second, r, step) in enumerate(pairs[p]):
+            form(slot, first, q, second, r)
+        made = jnp.dot(cross[...], table[...], preferred_element_type=F32)
+        mine[p] = made
+        leaving[p] = made.astype(BF)
+        row_copy(p).start()
+
+    def complete(p):
+        row_copy(p).wait_recv()
+        rows[pl.ds(p * 1024, 1024)] = (mine[p] + coming[p].astype(F32)).astype(BF)
+
+    def arrive(r):
+        for j in range(2):
+            far_copy(r, j).wait_recv()
+
+    arrive(FLIP)
+    for copy in table_copies:
+        copy.wait()
     correlate(0)
-    arrive(1)
+    arrive(BACK)
+    correlate(1)
     tally_stage(1)
-    arrive(3)
-    correlate(1)
-    arrive(2)
+    complete(0)
+    correlate(2)
+    for r in (FLIP, BACK, OPPOSITE):
+        far_code(r).wait_recv()
+    for p in range(4):
+        for slot, (first, q, second, r, step) in enumerate(pairs[p]):
+            from_row = pl.multiple_of((step - 1) * 256, 256)
+            spots[:, pl.ds(p * 1024 + slot * 256, 256)] = codes[first, q, :, pl.ds(from_row, 256)]
+    complete(1)
+    arrive(OPPOSITE)
+    correlate(3)
     tally_stage(2)
-    correlate(2)
 
     def place_of(code):
         slot = code % 64
@@ -232,11 +231,8 @@
         spot = (along * 4 + kind) * 256 + (first * 4 + second) * 16 + slot % 16
         return jnp.where(oc == core, spot, -1)
 
-    code_copy.wait_send()
-    codes[0] = place_of(codes[0])
-    codes[1] = place_of(codes[1])
-
-    correlate(3)
+    spots[...] = place_of(spots[...])
+    complete(2)
 
     def axis_of(kind):
         axis = kind - lax.div(kind, 3) * (3 - core)
@@ -249,25 +245,23 @@
         return send(dense.at[along, here], got_a.at[along, here], S_A + along * 4 + kind,
                     at(ex * along, ey * along, ez * along))
 
-    def group_half(along, half):
-        down = lax.broadcasted_iota(jnp.int32, (1024, 2048), 0)
-        hot = jnp.where(down == codes[half] - along * 1024, 1.0, 0.0).astype(BF)
-        return jnp.dot(hot, rows[half], preferred_element_type=F32)
-
-    own_sum[...] = group_half(2, 0)
-    for step in range(8):
-        row_copy(step)[1].wait_recv()
+    def group_of(along, begin, end):
+        down = lax.broadcasted_iota(jnp.int32, (1024, end - begin), 0)
+        hot = jnp.where(down == spots[:, begin:end] - along * 1024, 1.0, 0.0).astype(BF)
+        return jnp.dot(hot, rows[begin:end], preferred_element_type=F32)
 
     def send_group(along):
         for kind in range(4):
             copy_a(kind, along).start()
 
-    dense[2] = (own_sum[...] + group_half(2, 1)).astype(BF)
+    own_sum[...] = group_of(2, 0, 3072)
+    complete(3)
+    dense[2] = (own_sum[...] + group_of(2, 3072, 4096)).astype(BF)
     send_group(2)
     for along in (1, 3):
-        dense[along] = (group_half(along, 0) + group_half(along, 1)).astype(BF)
+        dense[along] = group_of(along, 0, 4096).astype(BF)
         send_group(along)
-    own_sum[...] = group_half(0, 0) + group_half(0, 1)
+    own_sum[...] = group_of(0, 0, 4096)
 
     def copy_b(kind, spot):
         ex, ey, ez = axis_of(kind)
@@ -303,14 +297,14 @@
     count = jnp.sum(jnp.where(diagonal, count, 0.0), axis=1, keepdims=True)
     scale = lax.rsqrt(count + 1.0)
 
-    for half in range(2):
-        flip(half).wait_send()
-        first_relay(half).wait_send()
-        for k in range(1, 4):
-            relay(k, half).wait_send()
-            along_z(k, half).wait_send()
-    for step in range(8):
-        row_copy(step)[1].wait_send()
+    sib_copy.wait_send()
+    code_copy.wait_send()
+    for r in (FLIP, BACK, OPPOSITE):
+        far_code(r).wait_send()
+        for j in range(2):
+            far_copy(r, j).wait_send()
+    for p in range(4):
+        row_copy(p).wait_send()
     for along in range(1, 4):
         for kind in range(4):
             copy_a(kind, along).wait_send()
@@ -335,13 +329,16 @@
                   pl.BlockSpec(memory_space=pl.ANY)],
         out_specs=vmem,
         scratch_shapes=[
-            pltpu.VMEM((2, CH, FREQS), BF),
-            pltpu.VMEM((2, CH, CH, FREQS), BF),
-            pltpu.VMEM((5, 2, 2, CH, FREQS), BF),
-            pltpu.VMEM((2 * FREQS, LAGS), BF),
-            pltpu.VMEM((512, 2 * FREQS), BF),
-            pltpu.VMEM((2, 2048, LAGS), BF),
-            pltpu.VMEM((2, 1, 2048), jnp.int32),
+            pltpu.VMEM((2, 2, CH, HALF), BF),
+            pltpu.VMEM((4, 2, 2, CH, HALF), BF),
+            pltpu.VMEM((FREQS, LAGS), BF),
+            pltpu.VMEM((1024, FREQS), BF),
+            pltpu.VMEM((4, 2, 1, 2048), jnp.int32),
+            pltpu.VMEM((1, 4096), jnp.int32),
+            pltpu.VMEM((4, 1024, LAGS), F32),
+            pltpu.VMEM((4, 1024, LAGS), BF),
+            pltpu.VMEM((4, 1024, LAGS), BF),
+            pltpu.VMEM((4096, LAGS), BF),
             pltpu.VMEM((1024, LAGS), F32),
             pltpu.VMEM((4, 1024, LAGS), BF),
             pltpu.VMEM((4, 1024, LAGS), BF),
@@ -351,7 +348,7 @@
             pltpu.VMEM((9, 32, 128), F32),
             pltpu.SemaphoreType.DMA((N_SEM,)),
             pltpu.SemaphoreType.DMA((N_SEM,)),
-            pltpu.SemaphoreType.DMA,
+            pltpu.SemaphoreType.DMA((2,)),
         ],
         compiler_params=pltpu.CompilerParams(
             collective_id=0, has_side_effects=True, vmem_limit_bytes=56 * 1024 * 1024),

time: 57.3 us -> 52.5 us (0.916)
  Pallas kernels: 55 us -> 49.9 us
    pallas_call x1, Pallas kernels: 55 us -> 49.9 us  [stacks(): pl.pallas_call(kernel, out_shape=jax.ShapeDtypeStruct((BINS_DEV, LAGS), F...]
where the time goes in v3:
time: 52.5 us; the launch traced here: 52.1 us
  Pallas kernels  49.9 us (95%)
  local copies, waits for them, and re-layouts  1.47 us (3%)
  between operations  0.66 us (1%)
    pallas_call x1, Pallas kernels, stacks(): pl.pallas_call(kernel, out_shape=jax.ShapeDtypeStruct((BINS_DEV, LAGS), F...  49.9 us
    unnamed x1, local copies, waits for them, and re-layouts  1.47 us

profile of v3, /device:TPU:0, one launch (start us, length us, event | category | flops | bytes accessed | tf_op | source)
XLA Modules:
  0.0 52.1 jit_solution(12084289673014009803)
XLA Ops:
  0.7 49.9 %shard_map.55 = f32[64,256]{1,0:T(8,128)} custom-call(bf16[16,2,2048]{2,1,0:T(2,128)(2,1)} %spec_ref.1, s32[1]{0:T(128)S(6)} %copy.7.live_ref, s32[1,2048]{1,0:T(1,128)} %bitcast.2, s32[1,2048]{1,0:T(1,128)} %bitcast.3, bf16[4096,256]{1,0:T(8,128)(2,1)} %constant.2.clone.table_hbm), custom_call_target="tpu_custom_call" | custom-call | flops 12999999488 | bytes 4000000 | tf_op jit(solution)/shard_map/pallas_call | solution.py:325
  50.6 1.5 %copy.8 = f32[64,256]{1,0:T(8,128)} copy(f32[64,256]{1,0:T(8,128)} %shard_map.55) | data formatting | bytes 131072

commit v4 on v3

--- a/solution.py
+++ b/solution.py
@@ -54,6 +54,9 @@
         return pltpu.make_async_remote_copy(
             src_ref=src, dst_ref=dst, send_sem=send_sem.at[number], recv_sem=recv_sem.at[number],
             device_id=device, device_id_type=MESH)
+
+    def apart(work):
+        pl.when(core < 2)(work)
 
     barrier = pltpu.get_barrier_semaphore()
     pl.semaphore_signal(barrier, inc=1, device_id=sibling, device_id_type=MESH)
@@ -147,7 +150,10 @@
         for v in range(1, 4):
             copy_n(stage, v).start()
 
-    tally[...] = hits_of(codes[OWN, 0]) + hits_of(codes[OWN, 1])
+    @apart
+    def _():
+        tally[...] = hits_of(codes[OWN, 0]) + hits_of(codes[OWN, 1])
+
     tally_stage(0)
 
     def pair_of(first, q, second, r, steps):
@@ -185,16 +191,21 @@
         return send(leaving.at[p], coming.at[p], S_ROWS + p, sibling)
 
     def correlate(p):
-        for slot, (first, q, second, r, step) in enumerate(pairs[p]):
-            form(slot, first, q, second, r)
-        made = jnp.dot(cross[...], table[...], preferred_element_type=F32)
-        mine[p] = made
-        leaving[p] = made.astype(BF)
+        @apart
+        def _():
+            for slot, (first, q, second, r, step) in enumerate(pairs[p]):
+                form(slot, first, q, second, r)
+            made = jnp.dot(cross[...], table[...], preferred_element_type=F32)
+            mine[p] = made
+            leaving[p] = made.astype(BF)
         row_copy(p).start()
 
     def complete(p):
         row_copy(p).wait_recv()
-        rows[pl.ds(p * 1024, 1024)] = (mine[p] + coming[p].astype(F32)).astype(BF)
+
+        @apart
+        def _():
+            rows[pl.ds(p * 1024, 1024)] = (mine[p] + coming[p].astype(F32)).astype(BF)
 
     def arrive(r):
         for j in range(2):
@@ -254,14 +265,27 @@
         for kind in range(4):
             copy_a(kind, along).start()
 
-    own_sum[...] = group_of(2, 0, 3072)
+    @apart
+    def _():
+        own_sum[...] = group_of(2, 0, 3072)
+
     complete(3)
-    dense[2] = (own_sum[...] + group_of(2, 3072, 4096)).astype(BF)
+
+    @apart
+    def _():
+        dense[2] = (own_sum[...] + group_of(2, 3072, 4096)).astype(BF)
+
     send_group(2)
     for along in (1, 3):
-        dense[along] = group_of(along, 0, 4096).astype(BF)
+        @apart
+        def _(along=along):
+            dense[along] = group_of(along, 0, 4096).astype(BF)
+
         send_group(along)
-    own_sum[...] = group_of(0, 0, 4096)
+
+    @apart
+    def _():
+        own_sum[...] = group_of(0, 0, 4096)
 
     def copy_b(kind, spot):
         ex, ey, ez = axis_of(kind)

time: 52.5 us -> 44.4 us (0.85)
  Pallas kernels: 49.9 us -> 42.1 us
    pallas_call x1, Pallas kernels: 49.9 us -> 42.1 us  [stacks(): pl.pallas_call(kernel, out_shape=jax.ShapeDtypeStruct((BINS_DEV, LAGS), F...]
where the time goes in v4:
time: 44.4 us; the launch traced here: 44.2 us
  Pallas kernels  42.1 us (95%)
  local copies, waits for them, and re-layouts  1.47 us (3%)
  between operations  0.66 us (1%)
    pallas_call x1, Pallas kernels, stacks(): pl.pallas_call(kernel, out_shape=jax.ShapeDtypeStruct((BINS_DEV, LAGS), F...  42.1 us
    unnamed x1, local copies, waits for them, and re-layouts  1.47 us

profile of v4, /device:TPU:0, one launch (start us, length us, event | category | flops | bytes accessed | tf_op | source)
XLA Modules:
  0.0 44.2 jit_solution(8356625872635300413)
XLA Ops:
  0.7 42.1 %shard_map.55 = f32[64,256]{1,0:T(8,128)} custom-call(bf16[16,2,2048]{2,1,0:T(2,128)(2,1)} %spec_ref.1, s32[1]{0:T(128)S(6)} %copy.7.live_ref, s32[1,2048]{1,0:T(1,128)} %bitcast.2, s32[1,2048]{1,0:T(1,128)} %bitcast.3, bf16[4096,256]{1,0:T(8,128)(2,1)} %constant.2.clone.table_hbm), custom_call_target="tpu_custom_call" | custom-call | flops 12999999488 | bytes 4000000 | tf_op jit(solution)/shard_map/pallas_call | solution.py:349
  42.7 1.5 %copy.8 = f32[64,256]{1,0:T(8,128)} copy(f32[64,256]{1,0:T(8,128)} %shard_map.55) | data formatting | bytes 131072

commit v5 on v4

--- a/solution.py
+++ b/solution.py
@@ -37,16 +37,20 @@
     return (x * 2 + lax.rem(y, 2), lax.div(y, 2) * 8 + z * 2 + core)
 
 
-def kernel(spec_ref, live_ref, owner_ref, bin_ref, table_hbm, out_ref, own, blocks, table, cross,
+def kernel(spec_hbm, live_ref, owner_hbm, bin_hbm, table_hbm, out_ref, spec, owner, bins, own, blocks, table, cross,
            codes, spots, mine, leaving, coming, rows, own_sum, dense, got_a, part, got_b, tally, got_n,
-           send_sem, recv_sem, table_sem):
+           send_sem, recv_sem, table_sem, in_sem):
     group, blk = lax.axis_index("group"), lax.axis_index("blk")
     mx, core = lax.div(group, 2), lax.rem(blk, 2)
     my = lax.div(blk, 8) * 2 + lax.rem(group, 2)
     mz = lax.rem(lax.div(blk, 2), 4)
 
+    part_x = [lax.rem(mx + v, 4) * 2 for v in range(4)]
+    part_y = [(lax.rem(lax.rem(my + v, 4), 2), lax.div(lax.rem(my + v, 4), 2) * 8) for v in range(4)]
+    part_z = [lax.rem(mz + v, 4) * 2 + core for v in range(4)]
+
     def at(dx, dy, dz):
-        return place(lax.rem(mx + dx, 4), lax.rem(my + dy, 4), lax.rem(mz + dz, 4), core)
+        return part_x[dx] + part_y[dy][0], part_y[dy][1] + part_z[dz]
 
     sibling = place(mx, my, mz, 1 - core)
 
@@ -63,6 +67,11 @@
     for v in range(1, 4):
         for device in (at(0, 0, v), at(0, v, 0), at(v, 0, 0)):
             pl.semaphore_signal(barrier, inc=1, device_id=device, device_id_type=MESH)
+
+    inputs = []
+    for number, pair in enumerate(((spec_hbm, spec), (owner_hbm, owner), (bin_hbm, bins))):
+        inputs.append(pltpu.make_async_copy(*pair, in_sem.at[number]))
+        inputs[number].start()
 
     table_copies = []
     for side in range(2):
@@ -71,7 +80,9 @@
             table_hbm.at[here], table.at[pl.ds(side * HALF, HALF)], table_sem.at[side]))
         table_copies[side].start()
 
-    values = spec_ref[...].astype(F32)
+    for copy in inputs:
+        copy.wait()
+    values = spec[...].astype(F32)
     real, imag = values[:, 0, :], values[:, 1, :]
     energy = real * real + imag * imag
     lane = lax.broadcasted_iota(jnp.int32, energy.shape, 1)
@@ -90,7 +101,7 @@
         for half in range(2):
             own[half, side] = white[:, half * HALF:(half + 1) * HALF]
     blocks[OWN, core] = own[core]
-    codes[OWN, core] = owner_ref[...] * BINS_DEV + bin_ref[...]
+    codes[OWN, core] = owner[...] * BINS_DEV + bins[...]
 
     pl.semaphore_wait(barrier, 10)
 
@@ -107,11 +118,11 @@
     def far_code(r):
         return send(codes.at[OWN], codes.at[r], S_CODE + r, toward[r])
 
-    for r in (FLIP, BACK, OPPOSITE):
-        far_copy(r, 0).start()
+    far_copy(FLIP, 0).start()
+    far_copy(BACK, 0).start()
     sib_copy.wait_recv()
-    for r in (FLIP, BACK, OPPOSITE):
-        far_copy(r, 1).start()
+    for r, j in ((FLIP, 1), (BACK, 1), (OPPOSITE, 0), (OPPOSITE, 1)):
+        far_copy(r, j).start()
     code_copy.wait_recv()
     for r in (FLIP, BACK, OPPOSITE):
         far_code(r).start()
@@ -217,7 +228,6 @@
     correlate(0)
     arrive(BACK)
     correlate(1)
-    tally_stage(1)
     complete(0)
     correlate(2)
     for r in (FLIP, BACK, OPPOSITE):
@@ -226,11 +236,6 @@
         for slot, (first, q, second, r, step) in enumerate(pairs[p]):
             from_row = pl.multiple_of((step - 1) * 256, 256)
             spots[:, pl.ds(p * 1024 + slot * 256, 256)] = codes[first, q, :, pl.ds(from_row, 256)]
-    complete(1)
-    arrive(OPPOSITE)
-    correlate(3)
-    tally_stage(2)
-
     def place_of(code):
         slot = code % 64
         dx, dy, dz, oc = offsets_of(code)
@@ -243,18 +248,23 @@
         return jnp.where(oc == core, spot, -1)
 
     spots[...] = place_of(spots[...])
+    tally_stage(1)
+    complete(1)
+    arrive(OPPOSITE)
+    correlate(3)
+    tally_stage(2)
     complete(2)
 
-    def axis_of(kind):
-        axis = kind - lax.div(kind, 3) * (3 - core)
-        ex, ez = lax.div(2 - axis, 2), lax.div(axis, 2)
-        return ex, 1 - ex - ez, ez
+    def device_of(kind, offsets):
+        if kind < 3:
+            return at(*offsets[kind])
+        one, other = at(*offsets[0]), at(*offsets[1])
+        return tuple(pick(core, b, a) for a, b in zip(one, other))
 
     def copy_a(kind, along):
-        ex, ey, ez = axis_of(kind)
-        here = pl.ds(pl.multiple_of(kind * 256, 256), 256)
+        here = pl.ds(kind * 256, 256)
         return send(dense.at[along, here], got_a.at[along, here], S_A + along * 4 + kind,
-                    at(ex * along, ey * along, ez * along))
+                    device_of(kind, ((along, 0, 0), (0, along, 0), (0, 0, along))))
 
     def group_of(along, begin, end):
         down = lax.broadcasted_iota(jnp.int32, (1024, end - begin), 0)
@@ -288,29 +298,28 @@
         own_sum[...] = group_of(0, 0, 4096)
 
     def copy_b(kind, spot):
-        ex, ey, ez = axis_of(kind)
-        first, second = lax.div(spot, 4), lax.rem(spot, 4)
-        dx = (1 - ex) * first
-        dy = ex * first + ez * second
-        dz = (1 - ez) * second
-        return send(part.at[kind, spot], got_b.at[kind, spot], S_B + kind, at(dx, dy, dz))
+        first, second = spot // 4, spot % 4
+        return send(part.at[kind, spot], got_b.at[kind, spot], S_B + kind,
+                    device_of(kind, ((0, first, second), (first, 0, second), (first, second, 0))))
 
     def all_b(kind):
         rest = pl.ds(1, 15)
         return send(part.at[kind, rest], got_b.at[kind, rest], S_B + kind, sibling)
 
     for kind in range(4):
-        here = pl.ds(kind * 256, 256)
-        total = own_sum[here]
         for along in (2, 1, 3):
             copy_a(kind, along).wait_recv()
-            total = total + got_a[along, here].astype(F32)
-        part[kind] = total.astype(BF).reshape(16, 16, LAGS)
-
-        def go(spot, carry, kind=kind):
+
+        @apart
+        def _(kind=kind):
+            here = pl.ds(kind * 256, 256)
+            total = own_sum[here]
+            for along in (2, 1, 3):
+                total = total + got_a[along, here].astype(F32)
+            part[kind] = total.astype(BF).reshape(16, 16, LAGS)
+
+        for spot in range(1, 16):
             copy_b(kind, spot).start()
-            return carry
-        lax.fori_loop(1, 16, go, 0)
 
     count = tally[0:1]
     for v in range(1, 4):
@@ -345,14 +354,16 @@
 
 
 def stacks(spectra, live_count, owner, slot, table):
-    vmem = pl.BlockSpec(memory_space=pltpu.VMEM)
+    vmem, anywhere = pl.BlockSpec(memory_space=pltpu.VMEM), pl.BlockSpec(memory_space=pl.ANY)
     return pl.pallas_call(
         kernel,
         out_shape=jax.ShapeDtypeStruct((BINS_DEV, LAGS), F32),
-        in_specs=[vmem, pl.BlockSpec(memory_space=pltpu.SMEM), vmem, vmem,
-                  pl.BlockSpec(memory_space=pl.ANY)],
+        in_specs=[anywhere, pl.BlockSpec(memory_space=pltpu.SMEM), anywhere, anywhere, anywhere],
         out_specs=vmem,
         scratch_shapes=[
+            pltpu.VMEM((CH, 2, FREQS), BF),
+            pltpu.VMEM((1, 2048), jnp.int32),
+            pltpu.VMEM((1, 2048), jnp.int32),
             pltpu.VMEM((2, 2, CH, HALF), BF),
             pltpu.VMEM((4, 2, 2, CH, HALF), BF),
             pltpu.VMEM((FREQS, LAGS), BF),
@@ -373,6 +384,7 @@
             pltpu.SemaphoreType.DMA((N_SEM,)),
             pltpu.SemaphoreType.DMA((N_SEM,)),
             pltpu.SemaphoreType.DMA((2,)),
+            pltpu.SemaphoreType.DMA((3,)),
         ],
         compiler_params=pltpu.CompilerParams(
             collective_id=0, has_side_effects=True, vmem_limit_bytes=56 * 1024 * 1024),

time: 44.4 us -> 44.4 us (level)
  no operation moved by 1% of the time
where the time goes in v5:
time: 44.4 us; the launch traced here: 44.2 us
  Pallas kernels  42.1 us (95%)
  local copies, waits for them, and re-layouts  1.47 us (3%)
  between operations  0.66 us (1%)
    pallas_call x1, Pallas kernels, stacks(): pl.pallas_call(kernel, out_shape=jax.ShapeDtypeStruct((BINS_DEV, LAGS), F...  42.1 us
    unnamed x1, local copies, waits for them, and re-layouts  1.47 us

profile of v5, /device:TPU:0, one launch (start us, length us, event | category | flops | bytes accessed | tf_op | source)
XLA Modules:
  0.0 44.2 jit_solution(16640902146780540043)
XLA Ops:
  0.7 42.1 %shard_map.55 = f32[64,256]{1,0:T(8,128)} custom-call(bf16[16,2,2048]{2,1,0:T(2,128)(2,1)} %spec_hbm.1, s32[1]{0:T(128)S(6)} %copy.7.live_ref, s32[1,2048]{1,0:T(1,128)} %bitcast.2, s32[1,2048]{1,0:T(1,128)} %bitcast.3, bf16[4096,256]{1,0:T(8,128)(2,1)} %constant.2.clone.table_hbm), custom_call_target="tpu_custom_call" | custom-call | flops 12999999488 | bytes 4000000 | tf_op jit(solution)/shard_map/pallas_call | solution.py:358
  42.7 1.5 %copy.8 = f32[64,256]{1,0:T(8,128)} copy(f32[64,256]{1,0:T(8,128)} %shard_map.55) | data formatting | bytes 131072

commit v6 on v5

--- a/solution.py
+++ b/solution.py
@@ -17,8 +17,8 @@
 BF = jnp.bfloat16
 F32 = jnp.float32
 
-S_SIB, S_FAR, S_CODE, S_ROWS, S_N, S_A, S_B = 0, 1, 7, 11, 15, 24, 40
-N_SEM = S_B + 4
+S_SIB, S_FAR, S_CODE, S_ROWS, S_N, S_A, S_B = 0, 1, 7, 11, 16, 25, 89
+N_SEM = S_B + 16
 OWN, BACK, OPPOSITE, FLIP = 0, 1, 2, 3
 HALF = FREQS // 2
 
@@ -38,7 +38,7 @@
 
 
 def kernel(spec_hbm, live_ref, owner_hbm, bin_hbm, table_hbm, out_ref, spec, owner, bins, own, blocks, table, cross,
-           codes, spots, mine, leaving, coming, rows, own_sum, dense, got_a, part, got_b, tally, got_n,
+           codes, spots, mine, leaving, coming, rows, early, own_sum, dense, got_a, part, got_b, tally, got_n,
            send_sem, recv_sem, table_sem, in_sem):
     group, blk = lax.axis_index("group"), lax.axis_index("blk")
     mx, core = lax.div(group, 2), lax.rem(blk, 2)
@@ -198,25 +198,36 @@
             cross[here, 0:HALF] = near_r * far_r + near_i * far_i
             cross[here, HALF:FREQS] = near_i * far_r - near_r * far_i
 
-    def row_copy(p):
-        return send(leaving.at[p], coming.at[p], S_ROWS + p, sibling)
-
-    def correlate(p):
+    runs = [(0, 0, 4), (1, 0, 4), (2, 0, 4), (3, 0, 2), (3, 2, 4)]
+
+    def row_copy(run):
+        p, begin, end = runs[run]
+        here = pl.ds(begin * 256, (end - begin) * 256)
+        return send(leaving.at[p, here], coming.at[p, here], S_ROWS + run, sibling)
+
+    def correlate(run):
+        p, begin, end = runs[run]
+        here = pl.ds(begin * 256, (end - begin) * 256)
+
         @apart
         def _():
-            for slot, (first, q, second, r, step) in enumerate(pairs[p]):
+            for slot in range(begin, end):
+                first, q, second, r, step = pairs[p][slot]
                 form(slot, first, q, second, r)
-            made = jnp.dot(cross[...], table[...], preferred_element_type=F32)
-            mine[p] = made
-            leaving[p] = made.astype(BF)
-        row_copy(p).start()
-
-    def complete(p):
-        row_copy(p).wait_recv()
+            made = jnp.dot(cross[here], table[...], preferred_element_type=F32)
+            mine[p, here] = made
+            leaving[p, here] = made.astype(BF)
+        row_copy(run).start()
+
+    def complete(run):
+        p, begin, end = runs[run]
+        here = pl.ds(begin * 256, (end - begin) * 256)
+        row_copy(run).wait_recv()
 
         @apart
         def _():
-            rows[pl.ds(p * 1024, 1024)] = (mine[p] + coming[p].astype(F32)).astype(BF)
+            total = mine[p, here] + coming[p, here].astype(F32)
+            rows[pl.ds(p * 1024 + begin * 256, (end - begin) * 256)] = total.astype(BF)
 
     def arrive(r):
         for j in range(2):
@@ -240,11 +251,12 @@
         slot = code % 64
         dx, dy, dz, oc = offsets_of(code)
         kind = slot // 16
-        axis = jnp.where(kind == 3, core, kind)
+        side = jnp.where(core == 0, dy, dx)
+        axis = jnp.where(kind == 3, jnp.where(side == 1, 2, core), kind)
+        first = jnp.where(kind == 3, side, jnp.where(kind == 0, dy, dx))
         along = jnp.where(axis == 0, dx, jnp.where(axis == 1, dy, dz))
-        first = jnp.where(axis == 0, dy, dx)
-        second = jnp.where(axis == 2, dy, dz)
-        spot = (along * 4 + kind) * 256 + (first * 4 + second) * 16 + slot % 16
+        second = jnp.where(axis < 2, dz, jnp.where((kind == 3) & (core == 0), dx, dy))
+        spot = first * 1024 + (along * 4 + kind) * 64 + second * 16 + slot % 16
         return jnp.where(oc == core, spot, -1)
 
     spots[...] = place_of(spots[...])
@@ -252,74 +264,91 @@
     complete(1)
     arrive(OPPOSITE)
     correlate(3)
+    correlate(4)
     tally_stage(2)
     complete(2)
 
     def device_of(kind, offsets):
         if kind < 3:
             return at(*offsets[kind])
-        one, other = at(*offsets[0]), at(*offsets[1])
+        one, other = at(*offsets[3]), at(*offsets[4])
         return tuple(pick(core, b, a) for a, b in zip(one, other))
 
-    def copy_a(kind, along):
-        here = pl.ds(kind * 256, 256)
-        return send(dense.at[along, here], got_a.at[along, here], S_A + along * 4 + kind,
-                    device_of(kind, ((along, 0, 0), (0, along, 0), (0, 0, along))))
-
-    def group_of(along, begin, end):
+    def copy_a(group, along, kind):
+        here = pl.ds(kind * 64, 64)
+        x, y, z = (along, 0, 0), (0, along, 0), (0, 0, along)
+        last = (z, z) if group == 1 else (x, y)
+        return send(dense.at[group, along, here], got_a.at[group, along, here],
+                    S_A + group * 16 + along * 4 + kind, device_of(kind, (x, y, z) + last))
+
+    def copy_b(group, kind, second):
+        if group == 1:
+            last = ((second, group, 0), (group, second, 0))
+        else:
+            last = ((0, group, second), (group, 0, second))
+        spot = kind * 4 + second
+        offsets = ((0, group, second), (group, 0, second), (group, second, 0)) + last
+        return send(part.at[group, spot], got_b.at[group, spot], S_B + group * 4 + kind,
+                    device_of(kind, offsets))
+
+    def all_b(group, kind):
+        skip = 1 if group == 0 else 0
+        here = pl.ds(kind * 4 + skip, 4 - skip)
+        return send(part.at[group, here], got_b.at[group, here], S_B + group * 4 + kind, sibling)
+
+    def hot_sum(group, begin, end):
         down = lax.broadcasted_iota(jnp.int32, (1024, end - begin), 0)
-        hot = jnp.where(down == spots[:, begin:end] - along * 1024, 1.0, 0.0).astype(BF)
+        hot = jnp.where(down == spots[:, begin:end] - group * 1024, 1.0, 0.0).astype(BF)
         return jnp.dot(hot, rows[begin:end], preferred_element_type=F32)
 
-    def send_group(along):
-        for kind in range(4):
-            copy_a(kind, along).start()
+    def keep(group, total):
+        own_sum[group] = total[0:256]
+        dense[group] = total.astype(BF).reshape(4, 256, LAGS)
+
+    def send_a(group):
+        for along in (2, 1, 3):
+            for kind in range(4):
+                copy_a(group, along, kind).start()
+
+    def pass_on(group):
+        for along in (2, 1, 3):
+            for kind in range(4):
+                copy_a(group, along, kind).wait_recv()
+
+        @apart
+        def _():
+            total = own_sum[group]
+            for along in (2, 1, 3):
+                total = total + got_a[group, along].astype(F32)
+            part[group] = total.astype(BF).reshape(16, 16, LAGS)
+
+        for second in range(4):
+            for kind in range(4):
+                if group or second:
+                    copy_b(group, kind, second).start()
 
     @apart
     def _():
-        own_sum[...] = group_of(2, 0, 3072)
+        early[...] = hot_sum(0, 0, 3072)
 
     complete(3)
+    complete(4)
 
     @apart
     def _():
-        dense[2] = (own_sum[...] + group_of(2, 3072, 4096)).astype(BF)
-
-    send_group(2)
-    for along in (1, 3):
+        keep(0, early[...] + hot_sum(0, 3072, 4096))
+
+    send_a(0)
+    for group in range(1, 4):
         @apart
-        def _(along=along):
-            dense[along] = group_of(along, 0, 4096).astype(BF)
-
-        send_group(along)
-
-    @apart
-    def _():
-        own_sum[...] = group_of(0, 0, 4096)
-
-    def copy_b(kind, spot):
-        first, second = spot // 4, spot % 4
-        return send(part.at[kind, spot], got_b.at[kind, spot], S_B + kind,
-                    device_of(kind, ((0, first, second), (first, 0, second), (first, second, 0))))
-
-    def all_b(kind):
-        rest = pl.ds(1, 15)
-        return send(part.at[kind, rest], got_b.at[kind, rest], S_B + kind, sibling)
-
-    for kind in range(4):
-        for along in (2, 1, 3):
-            copy_a(kind, along).wait_recv()
-
-        @apart
-        def _(kind=kind):
-            here = pl.ds(kind * 256, 256)
-            total = own_sum[here]
-            for along in (2, 1, 3):
-                total = total + got_a[along, here].astype(F32)
-            part[kind] = total.astype(BF).reshape(16, 16, LAGS)
-
-        for spot in range(1, 16):
-            copy_b(kind, spot).start()
+        def _(group=group):
+            keep(group, hot_sum(group, 0, 4096))
+
+        send_a(group)
+        if group == 3:
+            pass_on(0)
+    for group in range(1, 4):
+        pass_on(group)
 
     count = tally[0:1]
     for v in range(1, 4):
@@ -336,21 +365,32 @@
         far_code(r).wait_send()
         for j in range(2):
             far_copy(r, j).wait_send()
-    for p in range(4):
-        row_copy(p).wait_send()
-    for along in range(1, 4):
+    for run in range(5):
+        row_copy(run).wait_send()
+    for group in range(4):
+        for along in range(1, 4):
+            for kind in range(4):
+                copy_a(group, along, kind).wait_send()
+
+    def gather(group):
         for kind in range(4):
-            copy_a(kind, along).wait_send()
-
-    for kind in range(4):
-        all_b(kind).wait_recv()
-        total = part[kind, 0].astype(F32)
-        for spot in range(1, 16):
-            total = total + got_b[kind, spot].astype(F32)
-        out_ref[kind * 16:(kind + 1) * 16, :] = total * scale[kind * 16:(kind + 1) * 16]
-
-    for kind in range(4):
-        all_b(kind).wait_send()
+            all_b(group, kind).wait_recv()
+
+        @apart
+        def _():
+            for kind in range(4):
+                here = pl.ds(kind * 16, 16)
+                total = part[0, kind * 4].astype(F32) if group == 0 else out_ref[here]
+                for second in range(4):
+                    if group or second:
+                        total = total + got_b[group, kind * 4 + second].astype(F32)
+                out_ref[here] = total if group < 3 else total * scale[kind * 16:(kind + 1) * 16]
+
+    for group in range(4):
+        gather(group)
+    for group in range(4):
+        for kind in range(4):
+            all_b(group, kind).wait_send()
 
 
 def stacks(spectra, live_count, owner, slot, table):
@@ -375,8 +415,9 @@
             pltpu.VMEM((4, 1024, LAGS), BF),
             pltpu.VMEM((4096, LAGS), BF),
             pltpu.VMEM((1024, LAGS), F32),
-            pltpu.VMEM((4, 1024, LAGS), BF),
-            pltpu.VMEM((4, 1024, LAGS), BF),
+            pltpu.VMEM((4, 256, LAGS), F32),
+            pltpu.VMEM((4, 4, 256, LAGS), BF),
+            pltpu.VMEM((4, 4, 256, LAGS), BF),
             pltpu.VMEM((4, 16, 16, LAGS), BF),
             pltpu.VMEM((4, 16, 16, LAGS), BF),
             pltpu.VMEM((128, 128), F32),

time: 44.4 us -> 46.3 us (1.043)
  Pallas kernels: 42.1 us -> 43.7 us
    pallas_call x1, Pallas kernels: 42.1 us -> 43.7 us  [stacks(): pl.pallas_call(kernel, out_shape=jax.ShapeDtypeStruct((BINS_DEV, LAGS), F...]
where the time goes in v6:
time: 46.3 us; the launch traced here: 45.8 us
  Pallas kernels  43.7 us (94%)
  local copies, waits for them, and re-layouts  1.47 us (3%)
  between operations  0.66 us (1%)
    pallas_call x1, Pallas kernels, stacks(): pl.pallas_call(kernel, out_shape=jax.ShapeDtypeStruct((BINS_DEV, LAGS), F...  43.7 us
    unnamed x1, local copies, waits for them, and re-layouts  1.47 us

profile of v6, /device:TPU:0, one launch (start us, length us, event | category | flops | bytes accessed | tf_op | source)
XLA Modules:
  0.0 45.8 jit_solution(5898573716987614358)
XLA Ops:
  0.7 43.7 %shard_map.55 = f32[64,256]{1,0:T(8,128)} custom-call(bf16[16,2,2048]{2,1,0:T(2,128)(2,1)} %spec_hbm.1, s32[1]{0:T(128)S(6)} %copy.7.live_ref, s32[1,2048]{1,0:T(1,128)} %bitcast.2, s32[1,2048]{1,0:T(1,128)} %bitcast.3, bf16[4096,256]{1,0:T(8,128)(2,1)} %constant.2.clone.table_hbm), custom_call_target="tpu_custom_call" | custom-call | flops 12999999488 | bytes 4000000 | tf_op jit(solution)/shard_map/pallas_call | solution.py:398
  44.3 1.5 %copy.8 = f32[64,256]{1,0:T(8,128)} copy(f32[64,256]{1,0:T(8,128)} %shard_map.55) | data formatting | bytes 131072

commit v7 on v5

--- a/solution.py
+++ b/solution.py
@@ -17,7 +17,7 @@
 BF = jnp.bfloat16
 F32 = jnp.float32
 
-S_SIB, S_FAR, S_CODE, S_ROWS, S_N, S_A, S_B = 0, 1, 7, 11, 15, 24, 40
+S_SIB, S_FAR, S_CODE, S_ROWS, S_N, S_A, S_B = 0, 1, 7, 11, 27, 36, 56
 N_SEM = S_B + 4
 OWN, BACK, OPPOSITE, FLIP = 0, 1, 2, 3
 HALF = FREQS // 2
@@ -180,13 +180,26 @@
     cross_first, cross_second = pick(low, FLIP, BACK), pick(low, BACK, FLIP)
     far_first, far_second = pick(high, OWN, OPPOSITE), pick(high, OPPOSITE, OWN)
     flip_first, flip_second = pick(high, OPPOSITE, FLIP), pick(high, FLIP, OPPOSITE)
-    pairs = [
+    pairs = (
         [pair_of(OWN, 0, FLIP, 0, 8), pair_of(OWN, 0, FLIP, 1, 8),
-         pair_of(OWN, 1, FLIP, 1, 8), pair_of(OWN, 1, OWN, 0, 0)],
-        [pair_of(near_first, q, near_second, r, pick(low, 6, 2)) for q in (0, 1) for r in (0, 1)],
-        [pair_of(cross_first, q, cross_second, r, pick(low, 2, 6)) for q in (0, 1) for r in (0, 1)],
-        [pair_of(far_first, high, far_second, r, 4) for r in (0, 1)]
-        + [pair_of(flip_first, high, flip_second, r, 4) for r in (0, 1)],
+         pair_of(OWN, 1, FLIP, 1, 8), pair_of(OWN, 1, OWN, 0, 0)]
+        + [pair_of(near_first, q, near_second, r, pick(low, 6, 2)) for q in (0, 1) for r in (0, 1)]
+        + [pair_of(cross_first, q, cross_second, r, pick(low, 2, 6)) for q in (0, 1) for r in (0, 1)]
+        + [pair_of(far_first, high, far_second, r, 4) for r in (0, 1)]
+        + [pair_of(flip_first, high, flip_second, r, 4) for r in (0, 1)])
+
+    def near(mate, far):
+        q, r = pick(low, far, mate), pick(low, mate, far)
+        return 4 + 2 * q + r, (near_first, q, near_second, r)
+
+    def listed(number):
+        return number, pairs[number][:4]
+
+    runs = [
+        [listed(3), (core, (OWN, 0, FLIP, core)), near(0, core), near(1, core)],
+        [(1 - core, (OWN, 0, FLIP, 1 - core)), listed(2), near(0, 1 - core), near(1, 1 - core)],
+        [listed(number) for number in range(8, 12)],
+        [listed(number) for number in range(12, 16)],
     ]
 
     def form(slot, first, q, second, r):
@@ -198,73 +211,86 @@
             cross[here, 0:HALF] = near_r * far_r + near_i * far_i
             cross[here, HALF:FREQS] = near_i * far_r - near_r * far_i
 
-    def row_copy(p):
-        return send(leaving.at[p], coming.at[p], S_ROWS + p, sibling)
-
-    def correlate(p):
+    def row_copy(number):
+        return send(leaving.at[number], coming.at[number], S_ROWS + number, sibling)
+
+    def correlate(run):
         @apart
         def _():
-            for slot, (first, q, second, r, step) in enumerate(pairs[p]):
-                form(slot, first, q, second, r)
+            for slot, (number, pair) in enumerate(run):
+                form(slot, *pair)
             made = jnp.dot(cross[...], table[...], preferred_element_type=F32)
-            mine[p] = made
-            leaving[p] = made.astype(BF)
-        row_copy(p).start()
-
-    def complete(p):
-        row_copy(p).wait_recv()
+            for slot, (number, pair) in enumerate(run):
+                here = made[slot * 256:(slot + 1) * 256]
+                mine[number] = here
+                leaving[number] = here.astype(BF)
+        for number, pair in run:
+            row_copy(number).start()
+
+    def complete(begin, end):
+        for number in range(begin, end):
+            row_copy(number).wait_recv()
 
         @apart
         def _():
-            rows[pl.ds(p * 1024, 1024)] = (mine[p] + coming[p].astype(F32)).astype(BF)
-
-    def arrive(r):
-        for j in range(2):
-            far_copy(r, j).wait_recv()
-
-    arrive(FLIP)
+            for number in range(begin, end):
+                total = mine[number] + coming[number].astype(F32)
+                rows[number * 256:(number + 1) * 256] = total.astype(BF)
+
     for copy in table_copies:
         copy.wait()
-    correlate(0)
-    arrive(BACK)
-    correlate(1)
-    complete(0)
-    correlate(2)
-    for r in (FLIP, BACK, OPPOSITE):
-        far_code(r).wait_recv()
-    for p in range(4):
-        for slot, (first, q, second, r, step) in enumerate(pairs[p]):
-            from_row = pl.multiple_of((step - 1) * 256, 256)
-            spots[:, pl.ds(p * 1024 + slot * 256, 256)] = codes[first, q, :, pl.ds(from_row, 256)]
+    far_copy(FLIP, 0).wait_recv()
+    far_copy(BACK, 0).wait_recv()
+    correlate(runs[0])
+    far_copy(FLIP, 1).wait_recv()
+    far_copy(BACK, 1).wait_recv()
+    correlate(runs[1])
+    correlate(runs[2])
+    tally_stage(1)
+    far_copy(OPPOSITE, 0).wait_recv()
+    far_copy(OPPOSITE, 1).wait_recv()
+    correlate(runs[3])
+    tally_stage(2)
+
     def place_of(code):
         slot = code % 64
         dx, dy, dz, oc = offsets_of(code)
         kind = slot // 16
-        axis = jnp.where(kind == 3, core, kind)
+        side = jnp.where(core == 0, dy, dx)
+        axis = jnp.where(kind == 3, jnp.where(side == 3, 2, core), kind)
+        first = jnp.where(kind == 3, side, jnp.where(kind == 0, dy, dx))
         along = jnp.where(axis == 0, dx, jnp.where(axis == 1, dy, dz))
-        first = jnp.where(axis == 0, dy, dx)
-        second = jnp.where(axis == 2, dy, dz)
+        second = jnp.where(axis < 2, dz, jnp.where((kind == 3) & (core == 0), dx, dy))
         spot = (along * 4 + kind) * 256 + (first * 4 + second) * 16 + slot % 16
         return jnp.where(oc == core, spot, -1)
 
-    spots[...] = place_of(spots[...])
-    tally_stage(1)
-    complete(1)
-    arrive(OPPOSITE)
-    correlate(3)
-    tally_stage(2)
-    complete(2)
+    for r in (FLIP, BACK, OPPOSITE):
+        far_code(r).wait_recv()
+
+    @apart
+    def _():
+        for number, (first, q, second, r, step) in enumerate(pairs):
+            from_row = pl.multiple_of((step - 1) * 256, 256)
+            spots[:, number * 256:(number + 1) * 256] = codes[first, q, :, pl.ds(from_row, 256)]
+        spots[...] = place_of(spots[...])
+
+    complete(0, 12)
 
     def device_of(kind, offsets):
         if kind < 3:
             return at(*offsets[kind])
-        one, other = at(*offsets[0]), at(*offsets[1])
+        one, other = at(*offsets[3]), at(*offsets[4])
         return tuple(pick(core, b, a) for a, b in zip(one, other))
 
-    def copy_a(kind, along):
-        here = pl.ds(kind * 256, 256)
-        return send(dense.at[along, here], got_a.at[along, here], S_A + along * 4 + kind,
-                    device_of(kind, ((along, 0, 0), (0, along, 0), (0, 0, along))))
+    pieces = [(0, 0, 256), (1, 256, 256), (2, 512, 256), (3, 768, 192), (3, 960, 64)]
+
+    def copy_a(along, piece):
+        kind, begin, count = pieces[piece]
+        here = pl.ds(begin, count)
+        x, y, z = (along, 0, 0), (0, along, 0), (0, 0, along)
+        last = (z, z) if piece == 4 else (x, y)
+        return send(dense.at[along, here], got_a.at[along, here], S_A + along * 5 + piece,
+                    device_of(kind, (x, y, z) + last))
 
     def group_of(along, begin, end):
         down = lax.broadcasted_iota(jnp.int32, (1024, end - begin), 0)
@@ -272,14 +298,14 @@
         return jnp.dot(hot, rows[begin:end], preferred_element_type=F32)
 
     def send_group(along):
-        for kind in range(4):
-            copy_a(kind, along).start()
+        for piece in range(5):
+            copy_a(along, piece).start()
 
     @apart
     def _():
         own_sum[...] = group_of(2, 0, 3072)
 
-    complete(3)
+    complete(12, 16)
 
     @apart
     def _():
@@ -299,8 +325,9 @@
 
     def copy_b(kind, spot):
         first, second = spot // 4, spot % 4
-        return send(part.at[kind, spot], got_b.at[kind, spot], S_B + kind,
-                    device_of(kind, ((0, first, second), (first, 0, second), (first, second, 0))))
+        last = ((second, 3, 0), (3, second, 0)) if first == 3 else ((0, first, second), (first, 0, second))
+        offsets = ((0, first, second), (first, 0, second), (first, second, 0)) + last
+        return send(part.at[kind, spot], got_b.at[kind, spot], S_B + kind, device_of(kind, offsets))
 
     def all_b(kind):
         rest = pl.ds(1, 15)
@@ -308,7 +335,9 @@
 
     for kind in range(4):
         for along in (2, 1, 3):
-            copy_a(kind, along).wait_recv()
+            copy_a(along, kind).wait_recv()
+            if kind == 3:
+                copy_a(along, 4).wait_recv()
 
         @apart
         def _(kind=kind):
@@ -336,11 +365,11 @@
         far_code(r).wait_send()
         for j in range(2):
             far_copy(r, j).wait_send()
-    for p in range(4):
-        row_copy(p).wait_send()
+    for number in range(16):
+        row_copy(number).wait_send()
     for along in range(1, 4):
-        for kind in range(4):
-            copy_a(kind, along).wait_send()
+        for piece in range(5):
+            copy_a(along, piece).wait_send()
 
     for kind in range(4):
         all_b(kind).wait_recv()
@@ -370,9 +399,9 @@
             pltpu.VMEM((1024, FREQS), BF),
             pltpu.VMEM((4, 2, 1, 2048), jnp.int32),
             pltpu.VMEM((1, 4096), jnp.int32),
-            pltpu.VMEM((4, 1024, LAGS), F32),
-            pltpu.VMEM((4, 1024, LAGS), BF),
-            pltpu.VMEM((4, 1024, LAGS), BF),
+            pltpu.VMEM((16, 256, LAGS), F32),
+            pltpu.VMEM((16, 256, LAGS), BF),
+            pltpu.VMEM((16, 256, LAGS), BF),
             pltpu.VMEM((4096, LAGS), BF),
             pltpu.VMEM((1024, LAGS), F32),
             pltpu.VMEM((4, 1024, LAGS), BF),

time: 44.4 us -> 45.3 us (1.020)
  Pallas kernels: 42.1 us -> 43 us
    pallas_call x1, Pallas kernels: 42.1 us -> 43 us  [stacks(): pl.pallas_call(kernel, out_shape=jax.ShapeDtypeStruct((BINS_DEV, LAGS), F...]
where the time goes in v7:
time: 45.3 us; the launch traced here: 45.1 us
  Pallas kernels  43 us (95%)
  local copies, waits for them, and re-layouts  1.47 us (3%)
  between operations  0.66 us (1%)
    pallas_call x1, Pallas kernels, stacks(): pl.pallas_call(kernel, out_shape=jax.ShapeDtypeStruct((BINS_DEV, LAGS), F...  43 us
    unnamed x1, local copies, waits for them, and re-layouts  1.47 us

profile of v7, /device:TPU:0, one launch (start us, length us, event | category | flops | bytes accessed | tf_op | source)
XLA Modules:
  0.0 45.1 jit_solution(8823071983092323674)
XLA Ops:
  0.7 43.0 %shard_map.55 = f32[64,256]{1,0:T(8,128)} custom-call(bf16[16,2,2048]{2,1,0:T(2,128)(2,1)} %spec_hbm.1, s32[1]{0:T(128)S(6)} %copy.7.live_ref, s32[1,2048]{1,0:T(1,128)} %bitcast.2, s32[1,2048]{1,0:T(1,128)} %bitcast.3, bf16[4096,256]{1,0:T(8,128)(2,1)} %constant.2.clone.table_hbm), custom_call_target="tpu_custom_call" | custom-call | flops 12999999488 | bytes 4000000 | tf_op jit(solution)/shard_map/pallas_call | solution.py:387
  43.7 1.5 %copy.8 = f32[64,256]{1,0:T(8,128)} copy(f32[64,256]{1,0:T(8,128)} %shard_map.55) | data formatting | bytes 131072

commit v8 on v7

--- a/solution.py
+++ b/solution.py
@@ -17,8 +17,8 @@
 BF = jnp.bfloat16
 F32 = jnp.float32
 
-S_SIB, S_FAR, S_CODE, S_ROWS, S_N, S_A, S_B = 0, 1, 7, 11, 27, 36, 56
-N_SEM = S_B + 4
+S_SIB, S_FAR, S_CODE, S_ROWS, S_N, S_A, S_B = 0, 1, 7, 11, 27, 36, 66
+N_SEM = S_B + 8
 OWN, BACK, OPPOSITE, FLIP = 0, 1, 2, 3
 HALF = FREQS // 2
 
@@ -38,7 +38,7 @@
 
 
 def kernel(spec_hbm, live_ref, owner_hbm, bin_hbm, table_hbm, out_ref, spec, owner, bins, own, blocks, table, cross,
-           codes, spots, mine, leaving, coming, rows, own_sum, dense, got_a, part, got_b, tally, got_n,
+           codes, spots, mine, leaving, coming, rows, early, own_sum, dense, got_a, part, got_b, tally, got_n,
            send_sem, recv_sem, table_sem, in_sem):
     group, blk = lax.axis_index("group"), lax.axis_index("blk")
     mx, core = lax.div(group, 2), lax.rem(blk, 2)
@@ -121,8 +121,8 @@
     far_copy(FLIP, 0).start()
     far_copy(BACK, 0).start()
     sib_copy.wait_recv()
-    for r, j in ((FLIP, 1), (BACK, 1), (OPPOSITE, 0), (OPPOSITE, 1)):
-        far_copy(r, j).start()
+    for r in (FLIP, BACK):
+        far_copy(r, 1).start()
     code_copy.wait_recv()
     for r in (FLIP, BACK, OPPOSITE):
         far_code(r).start()
@@ -165,6 +165,9 @@
     def _():
         tally[...] = hits_of(codes[OWN, 0]) + hits_of(codes[OWN, 1])
 
+    far_copy(BACK, 1).wait_send()
+    for j in range(2):
+        far_copy(OPPOSITE, j).start()
     tally_stage(0)
 
     def pair_of(first, q, second, r, steps):
@@ -261,7 +264,7 @@
         first = jnp.where(kind == 3, side, jnp.where(kind == 0, dy, dx))
         along = jnp.where(axis == 0, dx, jnp.where(axis == 1, dy, dz))
         second = jnp.where(axis < 2, dz, jnp.where((kind == 3) & (core == 0), dx, dy))
-        spot = (along * 4 + kind) * 256 + (first * 4 + second) * 16 + slot % 16
+        spot = first // 2 * 2048 + (along * 4 + kind) * 128 + (first % 2 * 4 + second) * 16 + slot % 16
         return jnp.where(oc == core, spot, -1)
 
     for r in (FLIP, BACK, OPPOSITE):
@@ -282,73 +285,78 @@
         one, other = at(*offsets[3]), at(*offsets[4])
         return tuple(pick(core, b, a) for a, b in zip(one, other))
 
-    pieces = [(0, 0, 256), (1, 256, 256), (2, 512, 256), (3, 768, 192), (3, 960, 64)]
-
-    def copy_a(along, piece):
-        kind, begin, count = pieces[piece]
+    pieces = [[(0, 0, 128), (1, 128, 128), (2, 256, 128), (3, 384, 128)],
+              [(0, 0, 128), (1, 128, 128), (2, 256, 128), (3, 384, 64), (3, 448, 64)]]
+
+    def copy_a(half, along, piece):
+        kind, begin, count = pieces[half][piece]
         here = pl.ds(begin, count)
         x, y, z = (along, 0, 0), (0, along, 0), (0, 0, along)
         last = (z, z) if piece == 4 else (x, y)
-        return send(dense.at[along, here], got_a.at[along, here], S_A + along * 5 + piece,
-                    device_of(kind, (x, y, z) + last))
-
-    def group_of(along, begin, end):
-        down = lax.broadcasted_iota(jnp.int32, (1024, end - begin), 0)
-        hot = jnp.where(down == spots[:, begin:end] - along * 1024, 1.0, 0.0).astype(BF)
+        return send(dense.at[half, along, here], got_a.at[half, along, here],
+                    S_A + (half * 3 + along - 1) * 5 + piece, device_of(kind, (x, y, z) + last))
+
+    def group_of(half, along, begin, end):
+        down = lax.broadcasted_iota(jnp.int32, (512, end - begin), 0)
+        hot = jnp.where(down == spots[:, begin:end] - (half * 4 + along) * 512, 1.0, 0.0).astype(BF)
         return jnp.dot(hot, rows[begin:end], preferred_element_type=F32)
 
-    def send_group(along):
-        for piece in range(5):
-            copy_a(along, piece).start()
+    def send_group(half, along):
+        for piece in range(len(pieces[half])):
+            copy_a(half, along, piece).start()
 
     @apart
     def _():
-        own_sum[...] = group_of(2, 0, 3072)
+        early[0] = group_of(0, 2, 0, 3072)
+        early[1] = group_of(0, 1, 0, 3072)
 
     complete(12, 16)
+    for half, along in ((0, 2), (0, 1), (0, 3), (1, 2), (1, 1), (1, 3)):
+        @apart
+        def _(half=half, along=along):
+            if half == 0 and along < 3:
+                total = early[2 - along] + group_of(half, along, 3072, 4096)
+            else:
+                total = group_of(half, along, 0, 4096)
+            dense[half, along] = total.astype(BF)
+
+        send_group(half, along)
 
     @apart
     def _():
-        dense[2] = (own_sum[...] + group_of(2, 3072, 4096)).astype(BF)
-
-    send_group(2)
-    for along in (1, 3):
-        @apart
-        def _(along=along):
-            dense[along] = group_of(along, 0, 4096).astype(BF)
-
-        send_group(along)
-
-    @apart
-    def _():
-        own_sum[...] = group_of(0, 0, 4096)
+        for half in range(2):
+            own_sum[half] = group_of(half, 0, 0, 4096)
 
     def copy_b(kind, spot):
         first, second = spot // 4, spot % 4
         last = ((second, 3, 0), (3, second, 0)) if first == 3 else ((0, first, second), (first, 0, second))
         offsets = ((0, first, second), (first, 0, second), (first, second, 0)) + last
-        return send(part.at[kind, spot], got_b.at[kind, spot], S_B + kind, device_of(kind, offsets))
-
-    def all_b(kind):
-        rest = pl.ds(1, 15)
-        return send(part.at[kind, rest], got_b.at[kind, rest], S_B + kind, sibling)
-
-    for kind in range(4):
+        return send(part.at[kind, spot], got_b.at[kind, spot], S_B + kind * 2 + spot // 8,
+                    device_of(kind, offsets))
+
+    def all_b(kind, half):
+        here = pl.ds(1, 7) if half == 0 else pl.ds(8, 8)
+        return send(part.at[kind, here], got_b.at[kind, here], S_B + kind * 2 + half, sibling)
+
+    for half in range(2):
         for along in (2, 1, 3):
-            copy_a(along, kind).wait_recv()
-            if kind == 3:
-                copy_a(along, 4).wait_recv()
+            for piece in range(len(pieces[half])):
+                copy_a(half, along, piece).wait_recv()
 
         @apart
-        def _(kind=kind):
-            here = pl.ds(kind * 256, 256)
-            total = own_sum[here]
+        def _(half=half):
+            total = own_sum[half]
             for along in (2, 1, 3):
-                total = total + got_a[along, here].astype(F32)
-            part[kind] = total.astype(BF).reshape(16, 16, LAGS)
-
-        for spot in range(1, 16):
-            copy_b(kind, spot).start()
+                total = total + got_a[half, along].astype(F32)
+            total = total.astype(BF)
+            for kind in range(4):
+                here = total[kind * 128:(kind + 1) * 128]
+                part[kind, half * 8:half * 8 + 8] = here.reshape(8, 16, LAGS)
+
+        for spot in range(half * 8, half * 8 + 8):
+            for kind in range(4):
+                if spot:
+                    copy_b(kind, spot).start()
 
     count = tally[0:1]
     for v in range(1, 4):
@@ -364,22 +372,34 @@
     for r in (FLIP, BACK, OPPOSITE):
         far_code(r).wait_send()
         for j in range(2):
-            far_copy(r, j).wait_send()
+            if (r, j) != (BACK, 1):
+                far_copy(r, j).wait_send()
     for number in range(16):
         row_copy(number).wait_send()
-    for along in range(1, 4):
-        for piece in range(5):
-            copy_a(along, piece).wait_send()
-
-    for kind in range(4):
-        all_b(kind).wait_recv()
-        total = part[kind, 0].astype(F32)
-        for spot in range(1, 16):
-            total = total + got_b[kind, spot].astype(F32)
-        out_ref[kind * 16:(kind + 1) * 16, :] = total * scale[kind * 16:(kind + 1) * 16]
-
-    for kind in range(4):
-        all_b(kind).wait_send()
+    for half in range(2):
+        for along in range(1, 4):
+            for piece in range(len(pieces[half])):
+                copy_a(half, along, piece).wait_send()
+
+    def gather(half):
+        for kind in range(4):
+            all_b(kind, half).wait_recv()
+
+        @apart
+        def _():
+            for kind in range(4):
+                here = pl.ds(kind * 16, 16)
+                total = part[kind, 0].astype(F32) if half == 0 else out_ref[here]
+                for spot in range(half * 8, half * 8 + 8):
+                    if spot:
+                        total = total + got_b[kind, spot].astype(F32)
+                out_ref[here] = total if half == 0 else total * scale[kind * 16:(kind + 1) * 16]
+
+    for half in range(2):
+        gather(half)
+    for half in range(2):
+        for kind in range(4):
+            all_b(kind, half).wait_send()
 
 
 def stacks(spectra, live_count, owner, slot, table):
@@ -403,9 +423,10 @@
             pltpu.VMEM((16, 256, LAGS), BF),
             pltpu.VMEM((16, 256, LAGS), BF),
             pltpu.VMEM((4096, LAGS), BF),
-            pltpu.VMEM((1024, LAGS), F32),
-            pltpu.VMEM((4, 1024, LAGS), BF),
-            pltpu.VMEM((4, 1024, LAGS), BF),
+            pltpu.VMEM((2, 512, LAGS), F32),
+            pltpu.VMEM((2, 512, LAGS), F32),
+            pltpu.VMEM((2, 4, 512, LAGS), BF),
+            pltpu.VMEM((2, 4, 512, LAGS), BF),
             pltpu.VMEM((4, 16, 16, LAGS), BF),
             pltpu.VMEM((4, 16, 16, LAGS), BF),
             pltpu.VMEM((128, 128), F32),

time: 45.3 us -> 41.1 us (0.907)
  Pallas kernels: 43 us -> 38.7 us
    pallas_call x1, Pallas kernels: 43 us -> 38.7 us  [stacks(): pl.pallas_call(kernel, out_shape=jax.ShapeDtypeStruct((BINS_DEV, LAGS), F...]
where the time goes in v8:
time: 41.1 us; the launch traced here: 40.9 us
  Pallas kernels  38.7 us (94%)
  local copies, waits for them, and re-layouts  1.47 us (4%)
  between operations  0.66 us (2%)
    pallas_call x1, Pallas kernels, stacks(): pl.pallas_call(kernel, out_shape=jax.ShapeDtypeStruct((BINS_DEV, LAGS), F...  38.7 us
    unnamed x1, local copies, waits for them, and re-layouts  1.47 us

profile of v8, /device:TPU:0, one launch (start us, length us, event | category | flops | bytes accessed | tf_op | source)
XLA Modules:
  0.0 40.9 jit_solution(1780787362217621594)
XLA Ops:
  0.7 38.7 %shard_map.55 = f32[64,256]{1,0:T(8,128)} custom-call(bf16[16,2,2048]{2,1,0:T(2,128)(2,1)} %spec_hbm.1, s32[1]{0:T(128)S(6)} %copy.7.live_ref, s32[1,2048]{1,0:T(1,128)} %bitcast.2, s32[1,2048]{1,0:T(1,128)} %bitcast.3, bf16[4096,256]{1,0:T(8,128)(2,1)} %constant.2.clone.table_hbm), custom_call_target="tpu_custom_call" | custom-call | flops 12999999488 | bytes 4000000 | tf_op jit(solution)/shard_map/pallas_call | solution.py:407
  39.4 1.5 %copy.8 = f32[64,256]{1,0:T(8,128)} copy(f32[64,256]{1,0:T(8,128)} %shard_map.55) | data formatting | bytes 131072

commit v9 on v8

--- a/solution.py
+++ b/solution.py
@@ -202,7 +202,8 @@
         [listed(3), (core, (OWN, 0, FLIP, core)), near(0, core), near(1, core)],
         [(1 - core, (OWN, 0, FLIP, 1 - core)), listed(2), near(0, 1 - core), near(1, 1 - core)],
         [listed(number) for number in range(8, 12)],
-        [listed(number) for number in range(12, 16)],
+        [listed(number) for number in (12, 13)],
+        [listed(number) for number in (14, 15)],
     ]
 
     def form(slot, first, q, second, r):
@@ -222,7 +223,7 @@
         def _():
             for slot, (number, pair) in enumerate(run):
                 form(slot, *pair)
-            made = jnp.dot(cross[...], table[...], preferred_element_type=F32)
+            made = jnp.dot(cross[0:len(run) * 256], table[...], preferred_element_type=F32)
             for slot, (number, pair) in enumerate(run):
                 here = made[slot * 256:(slot + 1) * 256]
                 mine[number] = here
@@ -253,6 +254,7 @@
     far_copy(OPPOSITE, 0).wait_recv()
     far_copy(OPPOSITE, 1).wait_recv()
     correlate(runs[3])
+    correlate(runs[4])
     tally_stage(2)
 
     def place_of(code):
@@ -264,7 +266,8 @@
         first = jnp.where(kind == 3, side, jnp.where(kind == 0, dy, dx))
         along = jnp.where(axis == 0, dx, jnp.where(axis == 1, dy, dz))
         second = jnp.where(axis < 2, dz, jnp.where((kind == 3) & (core == 0), dx, dy))
-        spot = first // 2 * 2048 + (along * 4 + kind) * 128 + (first % 2 * 4 + second) * 16 + slot % 16
+        spot = jnp.where(first < 3, (along * 4 + kind) * 192 + first * 64,
+                         3072 + (along * 4 + kind) * 64) + second * 16 + slot % 16
         return jnp.where(oc == core, spot, -1)
 
     for r in (FLIP, BACK, OPPOSITE):
@@ -285,25 +288,28 @@
         one, other = at(*offsets[3]), at(*offsets[4])
         return tuple(pick(core, b, a) for a, b in zip(one, other))
 
-    pieces = [[(0, 0, 128), (1, 128, 128), (2, 256, 128), (3, 384, 128)],
-              [(0, 0, 128), (1, 128, 128), (2, 256, 128), (3, 384, 64), (3, 448, 64)]]
-
-    def copy_a(half, along, piece):
-        kind, begin, count = pieces[half][piece]
-        here = pl.ds(begin, count)
+    per_kind, begins = (192, 64), (0, 3072)
+
+    def copy_a(part_of, along, kind):
+        count = per_kind[part_of]
+        here = pl.ds(part_of * 768 + kind * count, count)
         x, y, z = (along, 0, 0), (0, along, 0), (0, 0, along)
-        last = (z, z) if piece == 4 else (x, y)
-        return send(dense.at[half, along, here], got_a.at[half, along, here],
-                    S_A + (half * 3 + along - 1) * 5 + piece, device_of(kind, (x, y, z) + last))
-
-    def group_of(half, along, begin, end):
-        down = lax.broadcasted_iota(jnp.int32, (512, end - begin), 0)
-        hot = jnp.where(down == spots[:, begin:end] - (half * 4 + along) * 512, 1.0, 0.0).astype(BF)
-        return jnp.dot(hot, rows[begin:end], preferred_element_type=F32)
-
-    def send_group(half, along):
-        for piece in range(len(pieces[half])):
-            copy_a(half, along, piece).start()
+        last = (z, z) if part_of else (x, y)
+        return send(dense.at[along, here], got_a.at[along, here],
+                    S_A + (part_of * 3 + along - 1) * 4 + kind, device_of(kind, (x, y, z) + last))
+
+    def group_of(part_of, along, begin, end):
+        size = 4 * per_kind[part_of]
+        down = lax.broadcasted_iota(jnp.int32, (size, end - begin), 0)
+        hot = jnp.where(down == spots[:, begin:end] - (begins[part_of] + along * size), 1.0, 0.0)
+        return jnp.dot(hot.astype(BF), rows[begin:end], preferred_element_type=F32)
+
+    def rows_of(part_of):
+        return pl.ds(0, 768) if part_of == 0 else pl.ds(768, 256)
+
+    def send_group(part_of, along):
+        for kind in range(4):
+            copy_a(part_of, along, kind).start()
 
     @apart
     def _():
@@ -311,52 +317,54 @@
         early[1] = group_of(0, 1, 0, 3072)
 
     complete(12, 16)
-    for half, along in ((0, 2), (0, 1), (0, 3), (1, 2), (1, 1), (1, 3)):
+    for part_of, along in ((0, 2), (0, 1), (0, 3), (1, 2), (1, 1), (1, 3)):
         @apart
-        def _(half=half, along=along):
-            if half == 0 and along < 3:
-                total = early[2 - along] + group_of(half, along, 3072, 4096)
+        def _(part_of=part_of, along=along):
+            if part_of == 0 and along < 3:
+                total = early[2 - along] + group_of(part_of, along, 3072, 4096)
             else:
-                total = group_of(half, along, 0, 4096)
-            dense[half, along] = total.astype(BF)
-
-        send_group(half, along)
+                total = group_of(part_of, along, 0, 4096)
+            dense[along, rows_of(part_of)] = total.astype(BF)
+
+        send_group(part_of, along)
 
     @apart
     def _():
-        for half in range(2):
-            own_sum[half] = group_of(half, 0, 0, 4096)
+        for part_of in range(2):
+            own_sum[rows_of(part_of)] = group_of(part_of, 0, 0, 4096)
 
     def copy_b(kind, spot):
         first, second = spot // 4, spot % 4
         last = ((second, 3, 0), (3, second, 0)) if first == 3 else ((0, first, second), (first, 0, second))
         offsets = ((0, first, second), (first, 0, second), (first, second, 0)) + last
-        return send(part.at[kind, spot], got_b.at[kind, spot], S_B + kind * 2 + spot // 8,
+        return send(part.at[kind, spot], got_b.at[kind, spot], S_B + kind * 2 + spot // 12,
                     device_of(kind, offsets))
 
-    def all_b(kind, half):
-        here = pl.ds(1, 7) if half == 0 else pl.ds(8, 8)
-        return send(part.at[kind, here], got_b.at[kind, here], S_B + kind * 2 + half, sibling)
-
-    for half in range(2):
+    spots_of = (range(1, 12), range(12, 16))
+
+    def all_b(kind, part_of):
+        here = pl.ds(spots_of[part_of][0], len(spots_of[part_of]))
+        return send(part.at[kind, here], got_b.at[kind, here], S_B + kind * 2 + part_of, sibling)
+
+    for part_of in range(2):
         for along in (2, 1, 3):
-            for piece in range(len(pieces[half])):
-                copy_a(half, along, piece).wait_recv()
+            for kind in range(4):
+                copy_a(part_of, along, kind).wait_recv()
 
         @apart
-        def _(half=half):
-            total = own_sum[half]
+        def _(part_of=part_of):
+            total = own_sum[rows_of(part_of)]
             for along in (2, 1, 3):
-                total = total + got_a[half, along].astype(F32)
+                total = total + got_a[along, rows_of(part_of)].astype(F32)
             total = total.astype(BF)
+            count = per_kind[part_of]
             for kind in range(4):
-                here = total[kind * 128:(kind + 1) * 128]
-                part[kind, half * 8:half * 8 + 8] = here.reshape(8, 16, LAGS)
-
-        for spot in range(half * 8, half * 8 + 8):
+                here = total[kind * count:(kind + 1) * count]
+                part[kind, pl.ds(part_of * 12, count // 16)] = here.reshape(count // 16, 16, LAGS)
+
+        for spot in spots_of[part_of]:
             for kind in range(4):
-                if spot:
-                    copy_b(kind, spot).start()
+                copy_b(kind, spot).start()
 
     count = tally[0:1]
     for v in range(1, 4):
@@ -376,30 +384,29 @@
                 far_copy(r, j).wait_send()
     for number in range(16):
         row_copy(number).wait_send()
-    for half in range(2):
+    for part_of in range(2):
         for along in range(1, 4):
-            for piece in range(len(pieces[half])):
-                copy_a(half, along, piece).wait_send()
-
-    def gather(half):
+            for kind in range(4):
+                copy_a(part_of, along, kind).wait_send()
+
+    def gather(part_of):
         for kind in range(4):
-            all_b(kind, half).wait_recv()
+            all_b(kind, part_of).wait_recv()
 
         @apart
         def _():
             for kind in range(4):
                 here = pl.ds(kind * 16, 16)
-                total = part[kind, 0].astype(F32) if half == 0 else out_ref[here]
-                for spot in range(half * 8, half * 8 + 8):
-                    if spot:
-                        total = total + got_b[kind, spot].astype(F32)
-                out_ref[here] = total if half == 0 else total * scale[kind * 16:(kind + 1) * 16]
-
-    for half in range(2):
-        gather(half)
-    for half in range(2):
+                total = out_ref[here] if part_of else part[kind, 0].astype(F32)
+                for spot in spots_of[part_of]:
+                    total = total + got_b[kind, spot].astype(F32)
+                out_ref[here] = total * scale[kind * 16:(kind + 1) * 16] if part_of else total
+
+    for part_of in range(2):
+        gather(part_of)
+    for part_of in range(2):
         for kind in range(4):
-            all_b(kind, half).wait_send()
+            all_b(kind, part_of).wait_send()
 
 
 def stacks(spectra, live_count, owner, slot, table):
@@ -423,10 +430,10 @@
             pltpu.VMEM((16, 256, LAGS), BF),
             pltpu.VMEM((16, 256, LAGS), BF),
             pltpu.VMEM((4096, LAGS), BF),
-            pltpu.VMEM((2, 512, LAGS), F32),
-            pltpu.VMEM((2, 512, LAGS), F32),
-            pltpu.VMEM((2, 4, 512, LAGS), BF),
-            pltpu.VMEM((2, 4, 512, LAGS), BF),
+            pltpu.VMEM((2, 768, LAGS), F32),
+            pltpu.VMEM((1024, LAGS), F32),
+            pltpu.VMEM((4, 1024, LAGS), BF),
+            pltpu.VMEM((4, 1024, LAGS), BF),
             pltpu.VMEM((4, 16, 16, LAGS), BF),
             pltpu.VMEM((4, 16, 16, LAGS), BF),
             pltpu.VMEM((128, 128), F32),

time: 41.1 us -> 42.9 us (1.044)
  the two profiles are of different devices: /device:TPU:0 before, /device:TPU:1 now
where the time goes in v9:
time: 42.9 us; the launch traced here: 42.7 us
  Pallas kernels  40.6 us (95%)
  local copies, waits for them, and re-layouts  1.47 us (3%)
  between operations  0.66 us (2%)
    pallas_call x1, Pallas kernels, stacks(): pl.pallas_call(kernel, out_shape=jax.ShapeDtypeStruct((BINS_DEV, LAGS), F...  40.6 us
    unnamed x1, local copies, waits for them, and re-layouts  1.47 us

profile of v9, /device:TPU:1, one launch (start us, length us, event | category | flops | bytes accessed | tf_op | source)
XLA Modules:
  0.0 42.7 jit_solution(6443545488759061085)
XLA Ops:
  0.7 40.6 %shard_map.55 = f32[64,256]{1,0:T(8,128)} custom-call(bf16[16,2,2048]{2,1,0:T(2,128)(2,1)} %spec_hbm.1, s32[1]{0:T(128)S(6)} %copy.7.live_ref, s32[1,2048]{1,0:T(1,128)} %bitcast.2, s32[1,2048]{1,0:T(1,128)} %bitcast.3, bf16[4096,256]{1,0:T(8,128)(2,1)} %constant.2.clone.table_hbm), custom_call_target="tpu_custom_call" | custom-call | flops 12999999488 | bytes 4000000 | tf_op jit(solution)/shard_map/pallas_call | solution.py:414
  41.2 1.5 %copy.8 = f32[64,256]{1,0:T(8,128)} copy(f32[64,256]{1,0:T(8,128)} %shard_map.55) | data formatting | bytes 131072

commit v10 on v9

--- a/solution.py
+++ b/solution.py
@@ -17,8 +17,8 @@
 BF = jnp.bfloat16
 F32 = jnp.float32
 
-S_SIB, S_FAR, S_CODE, S_ROWS, S_N, S_A, S_B = 0, 1, 7, 11, 27, 36, 66
-N_SEM = S_B + 8
+S_SIB, S_FAR, S_CODE, S_ROWS, S_N, S_A, S_B = 0, 1, 7, 11, 27, 36, 81
+N_SEM = S_B + 12
 OWN, BACK, OPPOSITE, FLIP = 0, 1, 2, 3
 HALF = FREQS // 2
 
@@ -202,8 +202,7 @@
         [listed(3), (core, (OWN, 0, FLIP, core)), near(0, core), near(1, core)],
         [(1 - core, (OWN, 0, FLIP, 1 - core)), listed(2), near(0, 1 - core), near(1, 1 - core)],
         [listed(number) for number in range(8, 12)],
-        [listed(number) for number in (12, 13)],
-        [listed(number) for number in (14, 15)],
+        [listed(number) for number in range(12, 16)],
     ]
 
     def form(slot, first, q, second, r):
@@ -223,7 +222,7 @@
         def _():
             for slot, (number, pair) in enumerate(run):
                 form(slot, *pair)
-            made = jnp.dot(cross[0:len(run) * 256], table[...], preferred_element_type=F32)
+            made = jnp.dot(cross[...], table[...], preferred_element_type=F32)
             for slot, (number, pair) in enumerate(run):
                 here = made[slot * 256:(slot + 1) * 256]
                 mine[number] = here
@@ -254,7 +253,6 @@
     far_copy(OPPOSITE, 0).wait_recv()
     far_copy(OPPOSITE, 1).wait_recv()
     correlate(runs[3])
-    correlate(runs[4])
     tally_stage(2)
 
     def place_of(code):
@@ -262,12 +260,15 @@
         dx, dy, dz, oc = offsets_of(code)
         kind = slot // 16
         side = jnp.where(core == 0, dy, dx)
-        axis = jnp.where(kind == 3, jnp.where(side == 3, 2, core), kind)
+        axis = jnp.where(kind == 3, jnp.where(side == 1, 2, core), kind)
         first = jnp.where(kind == 3, side, jnp.where(kind == 0, dy, dx))
         along = jnp.where(axis == 0, dx, jnp.where(axis == 1, dy, dz))
         second = jnp.where(axis < 2, dz, jnp.where((kind == 3) & (core == 0), dx, dy))
-        spot = jnp.where(first < 3, (along * 4 + kind) * 192 + first * 64,
-                         3072 + (along * 4 + kind) * 64) + second * 16 + slot % 16
+        order = jnp.where(along == 3, 2, 2 - along)
+        leave = jnp.where(first < 2, order * 512 + kind * 128 + first * 64,
+                          first * 768 + order * 256 + kind * 64)
+        stay = jnp.where(first < 2, 3072 + kind * 128 + first * 64, 3072 + first * 256 + kind * 64)
+        spot = jnp.where(along == 0, stay, leave) + second * 16 + slot % 16
         return jnp.where(oc == core, spot, -1)
 
     for r in (FLIP, BACK, OPPOSITE):
@@ -288,79 +289,83 @@
         one, other = at(*offsets[3]), at(*offsets[4])
         return tuple(pick(core, b, a) for a, b in zip(one, other))
 
-    per_kind, begins = (192, 64), (0, 3072)
-
-    def copy_a(part_of, along, kind):
-        count = per_kind[part_of]
-        here = pl.ds(part_of * 768 + kind * count, count)
+    begins, per_kind, stays = (0, 1536, 2304), (128, 64, 64), (0, 512, 768)
+    pieces = [[(0, 0, 128), (1, 128, 128), (2, 256, 128), (3, 384, 64), (3, 448, 64)],
+              [(kind, kind * 64, 64) for kind in range(4)]]
+
+    def rows_of(part_of, along):
+        count = 4 * per_kind[part_of]
+        return pl.ds(begins[part_of] + (2, 1, 3).index(along) * count, count)
+
+    def pieces_of(part_of):
+        return pieces[min(part_of, 1)]
+
+    def copy_a(part_of, along, piece):
+        kind, begin, count = pieces_of(part_of)[piece]
+        here = pl.ds(rows_of(part_of, along).start + begin, count)
         x, y, z = (along, 0, 0), (0, along, 0), (0, 0, along)
-        last = (z, z) if part_of else (x, y)
-        return send(dense.at[along, here], got_a.at[along, here],
-                    S_A + (part_of * 3 + along - 1) * 4 + kind, device_of(kind, (x, y, z) + last))
-
-    def group_of(part_of, along, begin, end):
-        size = 4 * per_kind[part_of]
-        down = lax.broadcasted_iota(jnp.int32, (size, end - begin), 0)
-        hot = jnp.where(down == spots[:, begin:end] - (begins[part_of] + along * size), 1.0, 0.0)
-        return jnp.dot(hot.astype(BF), rows[begin:end], preferred_element_type=F32)
-
-    def rows_of(part_of):
-        return pl.ds(0, 768) if part_of == 0 else pl.ds(768, 256)
-
-    def send_group(part_of, along):
-        for kind in range(4):
-            copy_a(part_of, along, kind).start()
+        last = (z, z) if piece == 4 else (x, y)
+        return send(dense.at[here], got_a.at[here], S_A + (part_of * 3 + along - 1) * 5 + piece,
+                    device_of(kind, (x, y, z) + last))
+
+    def group_of(base, begin, end):
+        down = lax.broadcasted_iota(jnp.int32, (512, end - begin), 0)
+        hot = jnp.where(down == spots[:, begin:end] - base, 1.0, 0.0).astype(BF)
+        return jnp.dot(hot, rows[begin:end], preferred_element_type=F32)
 
     @apart
     def _():
-        early[0] = group_of(0, 2, 0, 3072)
-        early[1] = group_of(0, 1, 0, 3072)
+        early[0] = group_of(0, 0, 3072)
+        early[1] = group_of(512, 0, 3072)
 
     complete(12, 16)
-    for part_of, along in ((0, 2), (0, 1), (0, 3), (1, 2), (1, 1), (1, 3)):
+    ready = [[(0, 2)], [(0, 1)], [(0, 3)], [(1, 2), (1, 1)], [(1, 3), (2, 2)], [(2, 1), (2, 3)]]
+    for group, leaves in enumerate(ready):
         @apart
-        def _(part_of=part_of, along=along):
-            if part_of == 0 and along < 3:
-                total = early[2 - along] + group_of(part_of, along, 3072, 4096)
+        def _(group=group):
+            if group < 2:
+                total = early[group] + group_of(group * 512, 3072, 4096)
             else:
-                total = group_of(part_of, along, 0, 4096)
-            dense[along, rows_of(part_of)] = total.astype(BF)
-
-        send_group(part_of, along)
+                total = group_of(group * 512, 0, 4096)
+            dense[pl.ds(group * 512, 512)] = total.astype(BF)
+
+        for part_of, along in leaves:
+            for piece in range(len(pieces_of(part_of))):
+                copy_a(part_of, along, piece).start()
 
     @apart
     def _():
-        for part_of in range(2):
-            own_sum[rows_of(part_of)] = group_of(part_of, 0, 0, 4096)
+        for half in range(2):
+            own_sum[pl.ds(half * 512, 512)] = group_of(3072 + half * 512, 0, 4096)
 
     def copy_b(kind, spot):
         first, second = spot // 4, spot % 4
-        last = ((second, 3, 0), (3, second, 0)) if first == 3 else ((0, first, second), (first, 0, second))
+        last = ((second, 1, 0), (1, second, 0)) if first == 1 else ((0, first, second), (first, 0, second))
         offsets = ((0, first, second), (first, 0, second), (first, second, 0)) + last
-        return send(part.at[kind, spot], got_b.at[kind, spot], S_B + kind * 2 + spot // 12,
+        return send(part.at[kind, spot], got_b.at[kind, spot], S_B + kind * 3 + max(spot // 4 - 1, 0),
                     device_of(kind, offsets))
 
-    spots_of = (range(1, 12), range(12, 16))
+    spots_of = (range(1, 8), range(8, 12), range(12, 16))
 
     def all_b(kind, part_of):
         here = pl.ds(spots_of[part_of][0], len(spots_of[part_of]))
-        return send(part.at[kind, here], got_b.at[kind, here], S_B + kind * 2 + part_of, sibling)
-
-    for part_of in range(2):
+        return send(part.at[kind, here], got_b.at[kind, here], S_B + kind * 3 + part_of, sibling)
+
+    for part_of in range(3):
         for along in (2, 1, 3):
-            for kind in range(4):
-                copy_a(part_of, along, kind).wait_recv()
+            for piece in range(len(pieces_of(part_of))):
+                copy_a(part_of, along, piece).wait_recv()
 
         @apart
         def _(part_of=part_of):
-            total = own_sum[rows_of(part_of)]
+            count = per_kind[part_of]
+            total = own_sum[pl.ds(stays[part_of], 4 * count)]
             for along in (2, 1, 3):
-                total = total + got_a[along, rows_of(part_of)].astype(F32)
+                total = total + got_a[rows_of(part_of, along)].astype(F32)
             total = total.astype(BF)
-            count = per_kind[part_of]
             for kind in range(4):
                 here = total[kind * count:(kind + 1) * count]
-                part[kind, pl.ds(part_of * 12, count // 16)] = here.reshape(count // 16, 16, LAGS)
+                part[kind, pl.ds(stays[part_of] // 64, count // 16)] = here.reshape(count // 16, 16, LAGS)
 
         for spot in spots_of[part_of]:
             for kind in range(4):
@@ -384,10 +389,10 @@
                 far_copy(r, j).wait_send()
     for number in range(16):
         row_copy(number).wait_send()
-    for part_of in range(2):
+    for part_of in range(3):
         for along in range(1, 4):
-            for kind in range(4):
-                copy_a(part_of, along, kind).wait_send()
+            for piece in range(len(pieces_of(part_of))):
+                copy_a(part_of, along, piece).wait_send()
 
     def gather(part_of):
         for kind in range(4):
@@ -400,11 +405,11 @@
                 total = out_ref[here] if part_of else part[kind, 0].astype(F32)
                 for spot in spots_of[part_of]:
                     total = total + got_b[kind, spot].astype(F32)
-                out_ref[here] = total * scale[kind * 16:(kind + 1) * 16] if part_of else total
-
-    for part_of in range(2):
+                out_ref[here] = total * scale[kind * 16:(kind + 1) * 16] if part_of == 2 else total
+
+    for part_of in range(3):
         gather(part_of)
-    for part_of in range(2):
+    for part_of in range(3):
         for kind in range(4):
             all_b(kind, part_of).wait_send()
 
@@ -430,10 +435,10 @@
             pltpu.VMEM((16, 256, LAGS), BF),
             pltpu.VMEM((16, 256, LAGS), BF),
             pltpu.VMEM((4096, LAGS), BF),
-            pltpu.VMEM((2, 768, LAGS), F32),
+            pltpu.VMEM((2, 512, LAGS), F32),
             pltpu.VMEM((1024, LAGS), F32),
-            pltpu.VMEM((4, 1024, LAGS), BF),
-            pltpu.VMEM((4, 1024, LAGS), BF),
+            pltpu.VMEM((3072, LAGS), BF),
+            pltpu.VMEM((3072, LAGS), BF),
             pltpu.VMEM((4, 16, 16, LAGS), BF),
             pltpu.VMEM((4, 16, 16, LAGS), BF),
             pltpu.VMEM((128, 128), F32),

time: 42.9 us -> 40.4 us (0.942)
  the two profiles are of different devices: /device:TPU:1 before, /device:TPU:0 now
where the time goes in v10:
time: 40.4 us; the launch traced here: 40.2 us
  Pallas kernels  38.1 us (94%)
  local copies, waits for them, and re-layouts  1.47 us (4%)
  between operations  0.66 us (2%)
    pallas_call x1, Pallas kernels, stacks(): pl.pallas_call(kernel, out_shape=jax.ShapeDtypeStruct((BINS_DEV, LAGS), F...  38.1 us
    unnamed x1, local copies, waits for them, and re-layouts  1.47 us

profile of v10, /device:TPU:0, one launch (start us, length us, event | category | flops | bytes accessed | tf_op | source)
XLA Modules:
  0.0 40.2 jit_solution(9483974913528368669)
XLA Ops:
  0.7 38.1 %shard_map.55 = f32[64,256]{1,0:T(8,128)} custom-call(bf16[16,2,2048]{2,1,0:T(2,128)(2,1)} %spec_hbm.1, s32[1]{0:T(128)S(6)} %copy.7.live_ref, s32[1,2048]{1,0:T(1,128)} %bitcast.2, s32[1,2048]{1,0:T(1,128)} %bitcast.3, bf16[4096,256]{1,0:T(8,128)(2,1)} %constant.2.clone.table_hbm), custom_call_target="tpu_custom_call" | custom-call | flops 12999999488 | bytes 4000000 | tf_op jit(solution)/shard_map/pallas_call | solution.py:419
  38.8 1.5 %copy.8 = f32[64,256]{1,0:T(8,128)} copy(f32[64,256]{1,0:T(8,128)} %shard_map.55) | data formatting | bytes 131072

commit v11 on v10

--- a/solution.py
+++ b/solution.py
@@ -250,11 +250,6 @@
     correlate(runs[1])
     correlate(runs[2])
     tally_stage(1)
-    far_copy(OPPOSITE, 0).wait_recv()
-    far_copy(OPPOSITE, 1).wait_recv()
-    correlate(runs[3])
-    tally_stage(2)
-
     def place_of(code):
         slot = code % 64
         dx, dy, dz, oc = offsets_of(code)
@@ -281,6 +276,10 @@
             spots[:, number * 256:(number + 1) * 256] = codes[first, q, :, pl.ds(from_row, 256)]
         spots[...] = place_of(spots[...])
 
+    far_copy(OPPOSITE, 0).wait_recv()
+    far_copy(OPPOSITE, 1).wait_recv()
+    correlate(runs[3])
+
     complete(0, 12)
 
     def device_of(kind, offsets):
@@ -332,6 +331,8 @@
         for part_of, along in leaves:
             for piece in range(len(pieces_of(part_of))):
                 copy_a(part_of, along, piece).start()
+        if group == 3:
+            tally_stage(2)
 
     @apart
     def _():
@@ -418,7 +419,7 @@
     vmem, anywhere = pl.BlockSpec(memory_space=pltpu.VMEM), pl.BlockSpec(memory_space=pl.ANY)
     return pl.pallas_call(
         kernel,
-        out_shape=jax.ShapeDtypeStruct((BINS_DEV, LAGS), F32),
+        out_shape=pltpu.VMEM((BINS_DEV, LAGS), F32),
         in_specs=[anywhere, pl.BlockSpec(memory_space=pltpu.SMEM), anywhere, anywhere, anywhere],
         out_specs=vmem,
         scratch_shapes=[

time: 40.4 us -> 38.8 us (0.960)
  Pallas kernels: 38.1 us -> 37 us
  local copies, waits for them, and re-layouts: 1.47 us -> 0.63 us
    pallas_call x1, Pallas kernels: 38.1 us -> 37 us  [stacks(): pl.pallas_call(kernel, out_shape=pltpu.VMEM((BINS_DEV, LAGS), F32), in_sp...]
    unnamed x1, local copies, waits for them, and re-layouts: 1.47 us -> 0.63 us
where the time goes in v11:
time: 38.8 us; the launch traced here: 38.3 us
  Pallas kernels  37 us (95%)
  between operations  0.66 us (2%)
  local copies, waits for them, and re-layouts  0.63 us (2%)
    pallas_call x1, Pallas kernels, stacks(): pl.pallas_call(kernel, out_shape=pltpu.VMEM((BINS_DEV, LAGS), F32), in_sp...  37 us

profile of v11, /device:TPU:0, one launch (start us, length us, event | category | flops | bytes accessed | tf_op | source)
XLA Modules:
  0.0 38.3 jit_solution(11489965186717371831)
XLA Ops:
  0.7 37.0 %shard_map.55 = f32[64,256]{1,0:T(8,128)S(1)} custom-call(bf16[16,2,2048]{2,1,0:T(2,128)(2,1)} %spec_hbm.1, s32[1]{0:T(128)S(6)} %copy.8.live_ref, s32[1,2048]{1,0:T(1,128)} %bitcast.2, s32[1,2048]{1,0:T(1,128)} %bitcast.3, bf16[4096,256]{1,0:T(8,128)(2,1)} %constant.2.clone.table_hbm), custom_call_target="tpu_custom_call" | custom-call | flops 12999999488 | bytes 4000000 | tf_op jit(solution)/shard_map/pallas_call | solution.py:420
  37.6 0.6 %copy.7 = f32[64,256]{1,0:T(8,128)} copy(f32[64,256]{1,0:T(8,128)S(1)} %shard_map.55) | data formatting | bytes 131072

commit v12 on v11

--- a/solution.py
+++ b/solution.py
@@ -118,10 +118,10 @@
     def far_code(r):
         return send(codes.at[OWN], codes.at[r], S_CODE + r, toward[r])
 
+    far_copy(BACK, 0).start()
     far_copy(FLIP, 0).start()
-    far_copy(BACK, 0).start()
     sib_copy.wait_recv()
-    for r in (FLIP, BACK):
+    for r in (BACK, FLIP):
         far_copy(r, 1).start()
     code_copy.wait_recv()
     for r in (FLIP, BACK, OPPOSITE):
@@ -276,11 +276,12 @@
             spots[:, number * 256:(number + 1) * 256] = codes[first, q, :, pl.ds(from_row, 256)]
         spots[...] = place_of(spots[...])
 
+    complete(0, 8)
     far_copy(OPPOSITE, 0).wait_recv()
     far_copy(OPPOSITE, 1).wait_recv()
     correlate(runs[3])
 
-    complete(0, 12)
+    complete(8, 12)
 
     def device_of(kind, offsets):
         if kind < 3:

time: 38.8 us -> 39 us (level)
  no operation moved by 1% of the time
where the time goes in v12:
time: 39 us; the launch traced here: 38.4 us
  Pallas kernels  37.1 us (95%)
  between operations  0.66 us (2%)
  local copies, waits for them, and re-layouts  0.63 us (2%)
    pallas_call x1, Pallas kernels, stacks(): pl.pallas_call(kernel, out_shape=pltpu.VMEM((BINS_DEV, LAGS), F32), in_sp...  37.1 us

profile of v12, /device:TPU:0, one launch (start us, length us, event | category | flops | bytes accessed | tf_op | source)
XLA Modules:
  0.0 38.4 jit_solution(16403006488842999482)
XLA Ops:
  0.7 37.1 %shard_map.55 = f32[64,256]{1,0:T(8,128)S(1)} custom-call(bf16[16,2,2048]{2,1,0:T(2,128)(2,1)} %spec_hbm.1, s32[1]{0:T(128)S(6)} %copy.8.live_ref, s32[1,2048]{1,0:T(1,128)} %bitcast.2, s32[1,2048]{1,0:T(1,128)} %bitcast.3, bf16[4096,256]{1,0:T(8,128)(2,1)} %constant.2.clone.table_hbm), custom_call_target="tpu_custom_call" | custom-call | flops 12999999488 | bytes 4000000 | tf_op jit(solution)/shard_map/pallas_call | solution.py:421
  37.8 0.6 %copy.7 = f32[64,256]{1,0:T(8,128)} copy(f32[64,256]{1,0:T(8,128)S(1)} %shard_map.55) | data formatting | bytes 131072
